TPU v7x, 512 devices: a whole 4x4x16 slice. The times are simulated.
512 devices in a mesh: feat: 16 (over x, y), label: 32 (over z, core).
Axes of the slice: x: 4, y: 4, z: 16, core: 2. Of those that a mesh axis runs over, the one named last changes fastest.
Arguments:
- doc_blocks: int32 [384, 8], replicated, may hold values from 0 to 511, all different within a row
- doc_counts: int32 [384], replicated, may hold values from 1 to 8
- doc_values: bfloat16 [384, 8, 256], replicated, may hold values from 0.049804688 to 2
- pos_labels: int32 [384, 8], replicated, may hold values from 0 to 131071, as said below
- neg_labels: int32 [384, 24], replicated, may hold values from 0 to 131071, as said below
- in_weight: bfloat16 [512, 256, 2048], P('feat', None, 'label'), may hold values from -0.1875 to 0.1875
- out_weight: bfloat16 [131072, 2048], P(('feat', 'label')), may hold values from -0.29882812 to 0.29882812
Outputs:
- in_grad: bfloat16 [512, 256, 2048], P('feat', None, 'label')
- out_grad: bfloat16 [131072, 2048], P(('feat', 'label'))
Inputs may be any that keep to these rules, and one draw needn't show every extreme that they name: The ids in one row of doc_blocks are distinct. `pos_labels`: label c is held by the device of linear index c // 256 (feat index times the size of label plus label index); taken together with neg_labels, every device's labels are named by exactly 24 of the listed pairs. `neg_labels`: see pos_labels.
All inputs are finite; a program needn't handle non-finite values.
Results may differ from a plain program's by a relative error of at most 0.0065.
Values may be sent and summed in bfloat16 or wider, within the bound.
No kernel may reach another device: no remote copies, remote signals or barrier semaphores. Data moves between devices by JAX's collectives and lax.ppermute only.
A program may use at most 128 MiB of HBM per device.

v0:
```python
import jax
import jax.numpy as jnp
from jax import lax
from jax.sharding import PartitionSpec as P


def on_device(doc_blocks, doc_counts, doc_values, pos_labels, neg_labels, in_weight, out_weight):
    block_count, block_size, col_count = in_weight.shape
    doc_total, slot_count = doc_blocks.shape
    lab_count = out_weight.shape[0]
    feat_index = lax.axis_index("feat")
    label_index = lax.axis_index("label")
    label_size = lax.axis_size("label")
    first_block = feat_index * block_count
    local_ids = doc_blocks - first_block
    slots = jnp.arange(slot_count, dtype=jnp.int32)
    valid = slots[None, :] < doc_counts[:, None]
    picks = (
        local_ids[:, :, None] == jnp.arange(block_count, dtype=jnp.int32)[None, None, :]
    ) & valid[:, :, None]
    dense = jnp.einsum(
        "dkb,dkv->dbv", picks.astype(jnp.bfloat16), doc_values, preferred_element_type=jnp.float32
    )
    flat_inputs = dense.astype(jnp.bfloat16).reshape(doc_total, block_count * block_size)
    weight_flat = in_weight.reshape(block_count * block_size, col_count)
    partial_value = jnp.dot(flat_inputs, weight_flat, preferred_element_type=jnp.float32)
    pre = lax.psum(partial_value, "feat")
    hidden_part = jax.nn.silu(pre).astype(jnp.bfloat16)
    hidden = lax.all_gather(hidden_part, "label", axis=1, tiled=True)
    logit = lax.dot_general(
        hidden, out_weight, (((1,), (1,)), ((), ())), preferred_element_type=jnp.float32
    )
    device_index = feat_index * label_size + label_index
    first_label = device_index * lab_count
    local_labels = jnp.arange(lab_count, dtype=jnp.int32)[None, None, :] + first_label
    pos_count = jnp.sum((pos_labels[:, :, None] == local_labels).astype(jnp.float32), axis=1)
    neg_count = jnp.sum((neg_labels[:, :, None] == local_labels).astype(jnp.float32), axis=1)
    sig = jax.nn.sigmoid(logit)
    grad_pos = (sig - 1.0).astype(jnp.bfloat16).astype(jnp.float32)
    grad_neg = sig.astype(jnp.bfloat16).astype(jnp.float32)
    label_grad = (pos_count * grad_pos + neg_count * grad_neg).astype(jnp.bfloat16)
    out_grad = lax.dot_general(
        label_grad, hidden, (((0,), (0,)), ((), ())), preferred_element_type=jnp.float32
    ).astype(jnp.bfloat16)
    grad_terms = jnp.dot(label_grad, out_weight, preferred_element_type=jnp.float32)
    summed = lax.psum(grad_terms, ("feat", "label"))
    hidden_grad = lax.dynamic_slice_in_dim(summed, label_index * col_count, col_count, 1)
    gate = jax.nn.sigmoid(pre)
    pre_grad = (hidden_grad * gate * (1.0 + pre * (1.0 - gate))).astype(jnp.bfloat16)
    in_flat = lax.dot_general(
        flat_inputs, pre_grad, (((0,), (0,)), ((), ())), preferred_element_type=jnp.float32
    )
    in_grad = in_flat.astype(jnp.bfloat16).reshape(block_count, block_size, col_count)
    return (in_grad, out_grad)


def solution(mesh):
    placed = (P(), P(), P(), P(), P(), P("feat", None, "label"), P(("feat", "label"), None))
    return jax.shard_map(
        on_device,
        mesh=mesh,
        in_specs=placed,
        out_specs=(P("feat", None, "label"), P(("feat", "label"), None)),
        check_vma=False,
    )
```

profile of v0, /device:TPU:1, one launch (start us, length us, event | category | flops | bytes accessed | tf_op | source)
XLA Modules:
  0.0 712.6 jit_solution(14605121180167996716)
XLA Ops:
  7.2 0.0 all-reduce.3.cloned.1.call-start
  7.2 0.8 broadcast_subtract_fusion
  8.1 0.1 copy.14
  8.2 0.8 iota_compare_fusion.1
  9.0 3.8 convolution_convert_fusion.1
  12.9 2.6 copy-done.1
  15.5 7.4 %fusion.7 = f32[384,64]{0,1:T(8,128)} fusion(bf16[32,256,64]{1,2,0:T(8,128)(2,1)S(1)} %copy-done.7, bf16[384,32,256]{2,1,0:T(8,128)(2,1)S(1)} %convolution_convert_fusion.1), kind=kOutput, calls=%fused_computation.13 | convolution fusion | flops 402653184 | bytes 7438336 | tf_op jit(solution)/shard_map/dot_general | solution.py:26
  22.9 0.0 all-gather.2.cloned.1.call-start
  23.0 116.5 %all-reduce.3.cloned.1.call-done = f32[384,64]{0,1:T(8,128)} async-done(((f32[384,64]{0,1:T(8,128)}), f32[384,64]{0,1:T(8,128)}) %all-reduce.3.cloned.1.call-update) | async-done | bytes 98320 | tf_op jit(solution)/shard_map/psum | solution.py:27
  139.5 1.6 multiply_convert_fusion.1
  141.0 0.0 all-gather.2.cloned.1.call-update
  141.1 0.0 all-reduce.5.cloned.1.call-start
  141.1 0.1 copy.17
  141.3 0.1 copy.15
  141.4 2.9 convert_reduce_fusion.1
  144.3 3.1 convert_reduce_fusion
  147.4 67.0 %all-gather.2.cloned.1.call-done = bf16[384,2048]{0,1:T(8,128)(2,1)} async-done(((bf16[384,64]{0,1:T(8,128)(2,1)}), bf16[384,2048]{0,1:T(8,128)(2,1)}) %all-gather.2.cloned.1.call-update) | async-done | bytes 1572880 | tf_op jit(solution)/shard_map/all_gather | solution.py:29
  214.4 2.2 add_convert_fusion
  216.7 2.4 fusion.15
  219.1 12.9 %copy.20 = bf16[48,8,32,256]{3,1,2,0:T(8,128)(2,1)} copy(bf16[48,8,32,256]{3,2,1,0:T(8,128)(2,1)} %bitcast.18) | data formatting | bytes 12582912
  232.0 1.7 convolution_convert_fusion.2
  233.7 467.2 %all-reduce.5.cloned.1.call-done = f32[384,2048]{0,1:T(8,128)} async-done(((f32[384,2048]{0,1:T(8,128)}), f32[384,2048]{0,1:T(8,128)}) %all-reduce.5.cloned.1.call-update) | async-done | bytes 3145744 | tf_op jit(solution)/shard_map/psum | solution.py:46
  700.9 4.1 convolution_convert_fusion
  705.0 1.1 copy.26
  (18 shorter events, 0.1 us)
Async XLA Ops:
  7.2 1.8 copy-start
  7.2 132.3 %all-reduce.3.cloned.1.call-start = ((), (), s32[]{:S(2)}) async-start(), calls=%async_computation | async-start | bytes 196608 | tf_op jit(solution)/shard_map/psum | solution.py:27
  9.0 6.5 copy-start.7
  12.8 2.6 copy-start.1
  15.5 125.6 %copy-start.5 = (s32[384,24]{0,1:T(8,128)S(1)}, s32[384,24]{0,1:T(8,128)}, u32[]{:S(2)}) copy-start(s32[384,24]{0,1:T(8,128)} %param.11) | copy-start | bytes 110596
  15.5 125.8 %copy-start.6 = (s32[384,8]{0,1:T(8,128)S(1)}, s32[384,8]{0,1:T(8,128)}, u32[]{:S(2)}) copy-start(s32[384,8]{0,1:T(8,128)} %param.10) | copy-start | bytes 36868
  15.5 198.9 %copy-start.3 = (bf16[256,2048]{1,0:T(8,128)(2,1)S(1)}, bf16[256,2048]{1,0:T(8,128)(2,1)}, u32[]{:S(2)}) copy-start(bf16[256,2048]{1,0:T(8,128)(2,1)} %param.13) | copy-start | bytes 3145732
  22.9 191.5 %all-gather.2.cloned.1.call-start = ((), (), s32[]{:S(2)}) async-start(), calls=%async_computation.1 | async-start | bytes 1622016 | tf_op jit(solution)/shard_map/all_gather | solution.py:29
  141.1 559.8 %all-reduce.5.cloned.1.call-start = ((), (), s32[]{:S(2)}) async-start(), calls=%async_computation.2 | async-start | bytes 6291456 | tf_op jit(solution)/shard_map/psum | solution.py:46
  219.1 12.9 %copy-start.2 = (bf16[384,2048]{0,1:T(8,128)(2,1)S(1)}, bf16[384,2048]{0,1:T(8,128)(2,1)}, u32[]{:S(2)}) copy-start(bf16[384,2048]{0,1:T(8,128)(2,1)} %all-gather.2.cloned.1.call-done) | copy-start | bytes 4718596
  219.1 481.8 %copy-start.4 = (f32[384,64]{0,1:T(8,128)S(1)}, f32[384,64]{0,1:T(8,128)}, u32[]{:S(2)}) copy-start(f32[384,64]{0,1:T(8,128)} %all-reduce.3.cloned.1.call-done) | copy-start | bytes 294916
Sparse Core Ops, SparseCore 0:
  23.1 116.3 all-reduce.2
  141.8 72.5 all-gather.1
  220.6 480.2 all-reduce.4
where the time goes:
time: 713 us
  waiting for transfers between devices  651 us (91%)
  matrix products  21.7 us (3%)
  local copies, waits for them, and re-layouts  17 us (2%)
  between operations  13.9 us (2%)
  other arithmetic  9.17 us (1%)
    psum x1, waiting for transfers between devices, on_device(): summed = lax.psum(grad_terms, ('feat', 'label'))  467 us
    psum x1, waiting for transfers between devices, on_device(): pre = lax.psum(partial_value, 'feat')  116 us
    all_gather x1, waiting for transfers between devices, on_device(): hidden = lax.all_gather(hidden_part, 'label', axis=1, tiled=True)  67 us
    unnamed x19, local copies, waits for them, and re-layouts  15.8 us
  transfers between devices with their start and end apart: 3, of which 3 were waited for; matrix products, arithmetic and copies ran while one was open for 3% of the time, Pallas kernels for 0%

commit v1 on v0

v1 whole, which is shorter than its diff:
```python
import jax
import jax.numpy as jnp
from jax import lax
from jax.sharding import PartitionSpec as P

F32 = jnp.float32
BF16 = jnp.bfloat16
ROWS = 32


def spread(part):
    shards = lax.axis_size("feat")
    copies = jnp.broadcast_to(part.astype(BF16)[None], (shards,) + part.shape)
    arrived = lax.all_to_all(copies, "feat", 0, 0, tiled=True)
    return jnp.sum(arrived.astype(F32), axis=0)


def on_device(doc_blocks, doc_counts, doc_values, pos_labels, neg_labels, in_weight, out_weight):
    block_count, block_size, col_count = in_weight.shape
    doc_total, slot_count = doc_blocks.shape
    lab_count, hidden_width = out_weight.shape
    feat_index = lax.axis_index("feat")
    label_index = lax.axis_index("label")
    owners = lax.axis_size("label")
    half = ROWS // 2

    local_ids = doc_blocks - feat_index * block_count
    slots = jnp.arange(slot_count, dtype=jnp.int32)
    valid = slots[None, :] < doc_counts[:, None]
    picks = (
        local_ids[:, :, None] == jnp.arange(block_count, dtype=jnp.int32)[None, None, :]
    ) & valid[:, :, None]
    dense = jnp.einsum(
        "dkb,dkv->dbv", picks.astype(BF16), doc_values, preferred_element_type=F32
    ).astype(BF16)
    weight_t = jnp.swapaxes(in_weight, 1, 2)
    partial_t = jnp.einsum("bhv,dbv->hd", weight_t, dense, preferred_element_type=F32)

    labels_t = jnp.concatenate([pos_labels.T, neg_labels.T], axis=0)
    rel = labels_t // lab_count - feat_index * owners
    count = jnp.sum(
        (rel[None] == jnp.arange(owners, dtype=jnp.int32)[:, None, None]).astype(F32), axis=1
    )
    docs = jnp.arange(doc_total, dtype=jnp.int32)
    before = (docs[:, None] < docs[None, :]).astype(BF16)
    base = jnp.dot(count.astype(BF16), before, preferred_element_type=F32)
    place = jnp.where(count > 0, base, -1.0)
    ranks = jnp.arange(ROWS, dtype=jnp.int32).astype(F32)
    pick_rows = (place[:, None, :] == ranks[None, :, None]).astype(BF16)
    pick_low = pick_rows[:, :half].reshape(owners * half, doc_total)
    pick_high = pick_rows[:, half:].reshape(owners * half, doc_total)

    pre_t = spread(partial_t)
    hidden_t = jax.nn.silu(pre_t).astype(BF16)
    nt = (((1,), (1,)), ((), ()))
    low = lax.dot_general(pick_low, hidden_t, nt, preferred_element_type=F32)
    high = lax.dot_general(pick_high, hidden_t, nt, preferred_element_type=F32)
    sent = jnp.concatenate([low, high], axis=1).astype(BF16).reshape(owners, half, 2 * col_count)
    got = lax.all_to_all(sent, "label", 0, 0, tiled=True)
    rows = got.reshape(owners, half, 2, col_count).transpose(2, 1, 0, 3).reshape(ROWS, hidden_width)

    logit = lax.dot_general(rows, out_weight, nt, preferred_element_type=F32)
    own = labels_t - (feat_index * owners + label_index) * lab_count
    own = jnp.where((own >= 0) & (own < lab_count), own + 1, 0).astype(BF16)
    own_place = lax.dynamic_slice_in_dim(place, label_index, 1, 0)
    own_pick = (own_place == ranks[:, None]).astype(BF16)
    row_labels = lax.dot_general(own_pick, own, nt, preferred_element_type=F32)
    names = jnp.arange(1, lab_count + 1, dtype=jnp.int32).astype(F32)
    hits = (row_labels[:, :, None] == names[None, None, :]).astype(F32)
    pos_slots = pos_labels.shape[1]
    pos_count = jnp.sum(hits[:, :pos_slots], axis=1)
    neg_count = jnp.sum(hits[:, pos_slots:], axis=1)
    sig = jax.nn.sigmoid(logit)
    grad_pos = (sig - 1.0).astype(BF16).astype(F32)
    grad_neg = sig.astype(BF16).astype(F32)
    label_grad = (pos_count * grad_pos + neg_count * grad_neg).astype(BF16)
    out_grad = lax.dot_general(
        label_grad, rows, (((0,), (0,)), ((), ())), preferred_element_type=F32
    ).astype(BF16)
    terms = jnp.dot(label_grad, out_weight, preferred_element_type=F32).astype(BF16)
    back = terms.reshape(2, half, owners, col_count).transpose(2, 1, 0, 3)
    back = back.reshape(owners, half, 2 * col_count)
    came = lax.all_to_all(back, "label", 0, 0, tiled=True).reshape(owners * half, 2 * col_count)
    tn = (((0,), (0,)), ((), ()))
    grad_part = lax.dot_general(
        came[:, :col_count], pick_low, tn, preferred_element_type=F32
    ) + lax.dot_general(came[:, col_count:], pick_high, tn, preferred_element_type=F32)

    hidden_grad = spread(grad_part)
    gate = jax.nn.sigmoid(pre_t)
    pre_grad = (hidden_grad * gate * (1.0 + pre_t * (1.0 - gate))).astype(BF16)
    in_grad = jnp.einsum("hd,dbv->bhv", pre_grad, dense, preferred_element_type=F32).astype(BF16)
    return (jnp.swapaxes(in_grad, 1, 2), out_grad)


def solution(mesh):
    placed = (P(), P(), P(), P(), P(), P("feat", None, "label"), P(("feat", "label"), None))
    return jax.shard_map(
        on_device,
        mesh=mesh,
        in_specs=placed,
        out_specs=(P("feat", None, "label"), P(("feat", "label"), None)),
        check_vma=False,
    )
```

time: 713 us -> 121 us (0.17)
  waiting for transfers between devices: 651 us -> 51.4 us
  starting transfers between devices: 0.12 us -> 36.2 us
  between operations: 13.9 us -> 0.95 us
  local copies, waits for them, and re-layouts: 17 us -> 4.41 us
    psum x2 -> x0, waiting for transfers between devices: 584 us -> none  [the longest x1 467 us: on_device(): summed = lax.psum(grad_terms, ('feat', 'label'))]
    all_gather x1 -> x0, waiting for transfers between devices: 67 us -> none  [on_device(): hidden = lax.all_gather(hidden_part, 'label', axis=1, tiled=True)]
    all_to_all x0 -> x4, waiting for transfers between devices: none -> 51.4 us  [the longest x2 21.1 us: spread(): arrived = lax.all_to_all(copies, 'feat', 0, 0, tiled=True)]
    all_to_all x0 -> x4, starting transfers between devices: none -> 36.2 us  [the longest x1 19.9 us: on_device(): got = lax.all_to_all(sent, 'label', 0, 0, tiled=True)]
    unnamed x19 -> x16, local copies, waits for them, and re-layouts: 15.8 us -> 0.37 us
    dot_general x6 -> x12, matrix products: 21.7 us -> 22.5 us  [the longest x1 7.57 us: on_device(): jnp.einsum('hd,dbv->bhv', pre_grad, dense, preferred_element_type=F32)]
  transfers between devices with their start and end apart: 3 -> 4, of which waited for: 3 -> 4; matrix products, arithmetic and copies ran while one was open for 3% -> 3% of each run, Pallas kernels for 0% -> 0%
where the time goes in v1:
time: 121 us; the launch traced here: 120 us
  waiting for transfers between devices  51.4 us (42%)
  starting transfers between devices  36.2 us (30%)
  matrix products  22.5 us (19%)
  other arithmetic  4.79 us (4%)
  local copies, waits for them, and re-layouts  4.41 us (4%)
    all_to_all x2, waiting for transfers between devices, spread(): arrived = lax.all_to_all(copies, 'feat', 0, 0, tiled=True)  21.1 us
    all_to_all x1, starting transfers between devices, on_device(): got = lax.all_to_all(sent, 'label', 0, 0, tiled=True)  19.9 us
    all_to_all x1, waiting for transfers between devices, on_device(): lax.all_to_all(back, 'label', 0, 0, tiled=True)  16.1 us
    all_to_all x1, waiting for transfers between devices, on_device(): got = lax.all_to_all(sent, 'label', 0, 0, tiled=True)  14.2 us
    all_to_all x2, starting transfers between devices, spread(): arrived = lax.all_to_all(copies, 'feat', 0, 0, tiled=True)  11.2 us
    dot_general x1, matrix products, on_device(): jnp.einsum('hd,dbv->bhv', pre_grad, dense, preferred_element_type=F32)  7.57 us
    dot_general x1, matrix products, on_device(): jnp.einsum('bhv,dbv->hd', weight_t, dense, preferred_element_type=F32)  6.78 us
    all_to_all x1, starting transfers between devices, on_device(): lax.all_to_all(back, 'label', 0, 0, tiled=True)  5.12 us
  transfers between devices with their start and end apart: 4, of which 4 were waited for; matrix products, arithmetic and copies ran while one was open for 3% of the time, Pallas kernels for 0%

profile of v1, /device:TPU:1, one launch (start us, length us, event | category | flops | bytes accessed | tf_op | source)
XLA Modules:
  0.0 120.2 jit_solution(12864910386003319441)
XLA Ops:
  0.7 0.8 broadcast_subtract_fusion
  1.6 0.8 iota_compare_fusion.4
  2.4 3.8 %convolution_convert_fusion = bf16[384,32,256]{2,1,0:T(8,128)(2,1)S(1)} fusion(bf16[384,8,256]{2,1,0:T(8,128)(2,1)S(1)} %copy-done, s32[384,8]{1,0:T(8,128)S(1)} %copy.17, pred[384,8]{1,0:T(8,128)(4,1)S(1)} %iota_compare_fusion.4), kind=kOutput, calls=%fused_computation.4 | convolution fusion | flops 53673984 | bytes 7879680 | tf_op jit(solution)/shard_map/dkb,dkv->dbv/dot_general | solution.py:33
  6.3 6.8 %fusion.16 = bf16[64,384]{1,0:T(8,128)(2,1)S(1)} fusion(bf16[384,32,256]{2,1,0:T(8,128)(2,1)S(1)} %convolution_convert_fusion, bf16[32,256,64]{1,2,0:T(8,128)(2,1)S(1)} %copy-done.7), kind=kOutput, calls=%fused_computation.20 | convolution fusion | flops 402677760 | bytes 7389184 | tf_op jit(solution)/shard_map/bhv,dbv->hd/dot_general | solution.py:37
  13.1 1.0 broadcast_in_dim.9
  14.1 7.6 %all-to-all-start = ((bf16[16,64,384]{2,1,0:T(8,128)(2,1)}), bf16[16,64,384]{2,1,0:T(8,128)(2,1)S(1)}, u32[]{:S(2)}, u32[]{:S(2)}) async-start(bf16[16,64,384]{2,1,0:T(8,128)(2,1)} %broadcast_in_dim.9), calls=%async_computation | async-start | bytes 1572864 | tf_op jit(solution)/shard_map/all_to_all | solution.py:14
  22.4 0.3 broadcast_compare_fusion
  22.7 9.7 %all-to-all-done = bf16[16,64,384]{2,1,0:T(8,128)(2,1)S(1)} async-done(((bf16[16,64,384]{2,1,0:T(8,128)(2,1)}), bf16[16,64,384]{2,1,0:T(8,128)(2,1)S(1)}, u32[]{:S(2)}, u32[]{:S(2)}) %all-to-all-start) | async-done | bytes 786464 | tf_op jit(solution)/shard_map/all_to_all | solution.py:14
  32.8 0.3 copy-done.3
  33.4 0.8 pad_maximum_fusion
  34.2 19.9 %all-to-all-start.1 = ((bf16[32,16,128]{2,1,0:T(8,128)(2,1)}), bf16[32,16,128]{2,1,0:T(8,128)(2,1)S(1)}, u32[]{:S(2)}, u32[]{:S(2)}) async-start(bf16[32,16,128]{2,1,0:T(8,128)(2,1)} %pad_maximum_fusion), calls=%async_computation.1 | async-start | bytes 262144 | tf_op jit(solution)/shard_map/all_to_all | solution.py:59
  54.3 0.7 slice_reduce_fusion.1
  55.0 0.7 slice_reduce_fusion
  55.7 14.2 %all-to-all-done.1 = bf16[32,16,128]{2,1,0:T(8,128)(2,1)S(1)} async-done(((bf16[32,16,128]{2,1,0:T(8,128)(2,1)}), bf16[32,16,128]{2,1,0:T(8,128)(2,1)S(1)}, u32[]{:S(2)}, u32[]{:S(2)}) %all-to-all-start.1) | async-done | bytes 131104 | tf_op jit(solution)/shard_map/all_to_all | solution.py:59
  70.4 1.2 %add_convert_fusion = bf16[32,256]{1,0:T(8,128)(2,1)S(1)} fusion(f32[32,256]{1,0:T(8,128)} %slice_reduce_fusion, f32[32,256]{1,0:T(8,128)} %slice_reduce_fusion.1, bf16[32,2048]{1,0:T(8,128)(2,1)S(1)} %reshape.138, bf16[256,2048]{1,0:T(8,128)(2,1)S(1)} %copy-done.2), kind=kOutput, calls=%fused_computation.59 | convolution fusion | flops 33652736 | bytes 1261568 | tf_op jit(solution)/shard_map/dot_general | solution.py:62
  72.5 0.8 reshape.140
  73.3 5.1 %all-to-all-start.2 = ((bf16[32,16,128]{2,1,0:T(8,128)(2,1)}), bf16[32,16,128]{2,1,0:T(8,128)(2,1)S(1)}, u32[]{:S(2)}, u32[]{:S(2)}) async-start(bf16[32,16,128]{2,1,0:T(8,128)(2,1)} %reshape.140), calls=%async_computation.2 | async-start | bytes 262144 | tf_op jit(solution)/shard_map/all_to_all | solution.py:83
  78.5 16.1 %all-to-all-done.2 = bf16[32,16,128]{2,1,0:T(8,128)(2,1)S(1)} async-done(((bf16[32,16,128]{2,1,0:T(8,128)(2,1)}), bf16[32,16,128]{2,1,0:T(8,128)(2,1)S(1)}, u32[]{:S(2)}, u32[]{:S(2)}) %all-to-all-start.2) | async-done | bytes 131104 | tf_op jit(solution)/shard_map/all_to_all | solution.py:83
  94.8 0.3 fusion.15
  95.2 1.0 broadcast_in_dim.11
  96.1 3.6 %all-to-all-start.3 = ((bf16[16,64,384]{2,1,0:T(8,128)(2,1)}), bf16[16,64,384]{2,1,0:T(8,128)(2,1)S(1)}, u32[]{:S(2)}, u32[]{:S(2)}) async-start(bf16[16,64,384]{2,1,0:T(8,128)(2,1)} %broadcast_in_dim.11), calls=%async_computation.3 | async-start | bytes 1572864 | tf_op jit(solution)/shard_map/all_to_all | solution.py:14
  99.8 1.4 %convolution_convert_fusion.1 = bf16[256,2048]{1,0:T(8,128)(2,1)} fusion(bf16[32,256]{1,0:T(8,128)(2,1)S(1)} %add_convert_fusion, bf16[32,2048]{1,0:T(8,128)(2,1)S(1)} %reshape.138), kind=kOutput, calls=%fused_computation.5 | convolution fusion | flops 34078720 | bytes 1196032 | tf_op jit(solution)/shard_map/dot_general | solution.py:77
  101.2 11.4 %all-to-all-done.3 = bf16[16,64,384]{2,1,0:T(8,128)(2,1)S(1)} async-done(((bf16[16,64,384]{2,1,0:T(8,128)(2,1)}), bf16[16,64,384]{2,1,0:T(8,128)(2,1)S(1)}, u32[]{:S(2)}, u32[]{:S(2)}) %all-to-all-start.3) | async-done | bytes 786464 | tf_op jit(solution)/shard_map/all_to_all | solution.py:14
  112.7 7.6 %fusion.6 = bf16[32,256,64]{1,2,0:T(8,128)(2,1)} fusion(bf16[384,32,256]{2,1,0:T(8,128)(2,1)} %copy-done.1, f32[64,384]{1,0:T(8,128)S(1)} %copy-done.4, f32[64,384]{1,0:T(8,128)S(1)} %convert_reduce_fusion), kind=kOutput, calls=%fused_computation.13 | convolution fusion | flops 403398656 | bytes 7536640 | tf_op jit(solution)/shard_map/hd,dbv->bhv/dot_general | solution.py:92
  (36 shorter events, 3.4 us)
Async XLA Ops:
  0.6 1.8 %copy-start = (bf16[384,8,256]{2,1,0:T(8,128)(2,1)S(1)}, bf16[384,8,256]{2,1,0:T(8,128)(2,1)}, u32[]{:S(2)}) copy-start(bf16[384,8,256]{2,1,0:T(8,128)(2,1)} %param.9) | copy-start | bytes 4718596
  2.4 3.8 %copy-start.7 = (bf16[32,256,64]{1,2,0:T(8,128)(2,1)S(1)}, bf16[32,256,64]{1,2,0:T(8,128)(2,1)}, u32[]{:S(2)}) copy-start(bf16[32,256,64]{1,2,0:T(8,128)(2,1)} %param.12) | copy-start | bytes 3145732
  6.3 6.8 %copy-start.1 = (bf16[384,32,256]{2,1,0:T(8,128)(2,1)}, bf16[384,32,256]{2,1,0:T(8,128)(2,1)S(1)}, u32[]{:S(2)}) copy-start(bf16[384,32,256]{2,1,0:T(8,128)(2,1)S(1)} %convolution_convert_fusion) | copy-start | bytes 18874372
  13.1 8.6 %copy-start.5 = (s32[384,24]{0,1:T(8,128)S(1)}, s32[384,24]{0,1:T(8,128)}, u32[]{:S(2)}) copy-start(s32[384,24]{0,1:T(8,128)} %param.11) | copy-start | bytes 110596
  13.1 8.6 %copy-start.6 = (s32[384,8]{0,1:T(8,128)S(1)}, s32[384,8]{0,1:T(8,128)}, u32[]{:S(2)}) copy-start(s32[384,8]{0,1:T(8,128)} %param.10) | copy-start | bytes 36868
  14.1 18.3 %all-to-all-start = ((bf16[16,64,384]{2,1,0:T(8,128)(2,1)}), bf16[16,64,384]{2,1,0:T(8,128)(2,1)S(1)}, u32[]{:S(2)}, u32[]{:S(2)}) async-start(bf16[16,64,384]{2,1,0:T(8,128)(2,1)} %broadcast_in_dim.9), calls=%async_computation | async-start | bytes 1572864 | tf_op jit(solution)/shard_map/all_to_all | solution.py:14
  32.5 0.6 copy-start.3
  33.4 37.0 %copy-start.2 = (bf16[256,2048]{1,0:T(8,128)(2,1)S(1)}, bf16[256,2048]{1,0:T(8,128)(2,1)}, u32[]{:S(2)}) copy-start(bf16[256,2048]{1,0:T(8,128)(2,1)} %param.13) | copy-start | bytes 3145732
  34.2 35.7 %all-to-all-start.1 = ((bf16[32,16,128]{2,1,0:T(8,128)(2,1)}), bf16[32,16,128]{2,1,0:T(8,128)(2,1)S(1)}, u32[]{:S(2)}, u32[]{:S(2)}) async-start(bf16[32,16,128]{2,1,0:T(8,128)(2,1)} %pad_maximum_fusion), calls=%async_computation.1 | async-start | bytes 262144 | tf_op jit(solution)/shard_map/all_to_all | solution.py:59
  73.3 21.3 %all-to-all-start.2 = ((bf16[32,16,128]{2,1,0:T(8,128)(2,1)}), bf16[32,16,128]{2,1,0:T(8,128)(2,1)S(1)}, u32[]{:S(2)}, u32[]{:S(2)}) async-start(bf16[32,16,128]{2,1,0:T(8,128)(2,1)} %reshape.140), calls=%async_computation.2 | async-start | bytes 262144 | tf_op jit(solution)/shard_map/all_to_all | solution.py:83
  95.1 17.5 %copy-start.4 = (f32[64,384]{1,0:T(8,128)S(1)}, f32[64,384]{1,0:T(8,128)}, u32[]{:S(2)}) copy-start(f32[64,384]{1,0:T(8,128)} %copy-done.3) | copy-start | bytes 294916
  96.1 16.4 %all-to-all-start.3 = ((bf16[16,64,384]{2,1,0:T(8,128)(2,1)}), bf16[16,64,384]{2,1,0:T(8,128)(2,1)S(1)}, u32[]{:S(2)}, u32[]{:S(2)}) async-start(bf16[16,64,384]{2,1,0:T(8,128)(2,1)} %broadcast_in_dim.11), calls=%async_computation.3 | async-start | bytes 1572864 | tf_op jit(solution)/shard_map/all_to_all | solution.py:14

commit v2 on v1

v2 whole, which is shorter than its diff:
```python
import jax
import jax.numpy as jnp
from jax import lax
from jax.experimental import pallas as pl
from jax.experimental.pallas import tpu as pltpu
from jax.sharding import PartitionSpec as P

F32 = jnp.float32
BF16 = jnp.bfloat16
ROWS = 32


GROUP = 32
CHUNK = 256
NOTES = 16
VMEM = pl.BlockSpec(memory_space=pltpu.VMEM)
SMEM = pl.BlockSpec(memory_space=pltpu.SMEM)
HBM = pl.BlockSpec(memory_space=pltpu.HBM)
NT = (((1,), (1,)), ((), ()))


def iota(shape, dim):
    return lax.broadcasted_iota(jnp.int32, shape, dim)


def one_hot(left, right):
    return jnp.where(left == right, 1.0, 0.0).astype(BF16)


def owner_rows(notes, docs):
    held = notes.astype(F32)
    doc = held[2:3] * float(GROUP) + held[1:2]
    return one_hot(iota((docs, 1), 0).astype(F32), doc), held[0:1]


def forward_kernel(
    code_hbm, values_hbm, weight_hbm, packed_hbm, count_ref, out_ref,
    code_ref, values, weight, rank_ref, stage, total_ref, sems, weight_sem, stage_sem,
):
    groups = values.shape[0]
    blocks, cols, width = weight.shape
    docs = groups * GROUP
    code_load = pltpu.make_async_copy(code_hbm, code_ref, stage_sem)
    code_load.start()
    loads = [
        pltpu.make_async_copy(values_hbm.at[g], values.at[g], sems.at[g]) for g in range(groups)
    ]
    for load in loads:
        load.start()
    weight_load = pltpu.make_async_copy(weight_hbm, weight, weight_sem)
    weight_load.start()

    code_load.wait()
    code = code_ref[...].astype(F32)
    pad_groups, lanes = code.shape
    listed = jnp.where(code >= 0.0, 1.0, 0.0)
    listed16 = listed.astype(BF16)
    ahead = jnp.where(iota((lanes, lanes), 0) < iota((lanes, lanes), 1), 1.0, 0.0).astype(BF16)
    above = jnp.where(
        iota((pad_groups, pad_groups), 0) > iota((pad_groups, pad_groups), 1), 1.0, 0.0
    ).astype(BF16)
    upper = jnp.dot(above, listed16, preferred_element_type=F32).astype(BF16)
    rank = jnp.dot(listed16, ahead, preferred_element_type=F32) + jnp.dot(
        upper, jnp.ones((lanes, lanes), BF16), preferred_element_type=F32
    )
    rank_ref[...] = jnp.where(code >= 0.0, rank, -1.0)
    count = jnp.sum(listed).astype(jnp.int32)
    chunks = jnp.maximum((count + CHUNK - 1) // CHUNK, 1)
    count_ref[0, 0] = chunks
    note_row = iota((NOTES, lanes), 0)
    lane_doc = (iota((NOTES, lanes), 1) // (lanes // GROUP)).astype(F32)

    def add_chunk(chunk, wait):
        spots = (iota((CHUNK, 1), 0) + chunk * CHUNK).astype(F32)
        rows = jnp.zeros((CHUNK, width), F32)
        notes = jnp.zeros((NOTES, CHUNK), F32)
        for g in range(groups):
            pick = one_hot(spots, rank_ref[g : g + 1])
            told = jnp.where(note_row == 0, code_ref[g : g + 1].astype(F32), 0.0)
            told = jnp.where(note_row == 1, lane_doc, told)
            told = jnp.where(note_row == 2, float(g), told).astype(BF16)
            notes += lax.dot_general(told, pick, NT, preferred_element_type=F32)
            if wait:
                loads[g].wait()
            rows += jnp.dot(pick, values[g], preferred_element_type=F32)
        stage[:CHUNK] = rows.astype(BF16)
        stage[CHUNK:] = notes.astype(BF16)
        save = pltpu.make_async_copy(stage, packed_hbm.at[chunk], stage_sem)
        save.start()
        doc_rows, block = owner_rows(stage[CHUNK:], docs)
        if wait:
            weight_load.wait()
        every = lax.dot_general(
            weight[...].reshape(blocks * cols, width), stage[:CHUNK], NT, preferred_element_type=F32
        )
        part = jnp.zeros((cols, CHUNK), F32)
        for b in range(blocks):
            part += jnp.where(block == float(b), every[b * cols : (b + 1) * cols], 0.0)
        high = part.astype(BF16)
        low = (part - high.astype(F32)).astype(BF16)
        both = lax.dot_general(
            jnp.concatenate([high, low], axis=0), doc_rows, NT, preferred_element_type=F32
        )
        save.wait()
        return both[:cols] + both[cols:]

    total_ref[...] = add_chunk(0, True)

    @pl.when(chunks > 1)
    def _():
        @pl.loop(1, chunks)
        def _(chunk):
            total_ref[...] += add_chunk(chunk, False)

    part = total_ref[...].astype(BF16)
    for shard in range(out_ref.shape[0]):
        out_ref[shard] = part


def forward(code, values, weight_t, shards):
    blocks, cols, width = weight_t.shape
    groups, lanes, _ = values.shape
    docs = groups * GROUP
    most = -(-groups * lanes // CHUNK)
    return pl.pallas_call(
        forward_kernel,
        out_shape=(
            jax.ShapeDtypeStruct((most, CHUNK + NOTES, width), BF16),
            jax.ShapeDtypeStruct((1, 1), jnp.int32),
            jax.ShapeDtypeStruct((shards, cols, docs), BF16),
        ),
        in_specs=[HBM, HBM, HBM],
        out_specs=(HBM, SMEM, VMEM),
        scratch_shapes=[
            pltpu.VMEM(code.shape, jnp.int32),
            pltpu.VMEM(values.shape, BF16),
            pltpu.VMEM(weight_t.shape, BF16),
            pltpu.VMEM(code.shape, F32),
            pltpu.VMEM((CHUNK + NOTES, width), BF16),
            pltpu.VMEM((cols, docs), F32),
            pltpu.SemaphoreType.DMA((groups,)),
            pltpu.SemaphoreType.DMA(()),
            pltpu.SemaphoreType.DMA(()),
        ],
        compiler_params=pltpu.CompilerParams(vmem_limit_bytes=60 << 20),
    )(code, values, weight_t)


def backward_kernel(count_ref, parts_ref, pre_ref, packed_hbm, out_ref, stage, grad_ref, total_ref, sem):
    blocks, cols, width = out_ref.shape
    docs = pre_ref.shape[1]
    chunks = count_ref[0, 0]
    first = pltpu.make_async_copy(packed_hbm.at[0], stage, sem)
    first.start()
    hidden_grad = parts_ref[0].astype(F32)
    for shard in range(1, parts_ref.shape[0]):
        hidden_grad += parts_ref[shard].astype(F32)
    pre = pre_ref[...]
    gate = jax.nn.sigmoid(pre)
    grad_ref[...] = (hidden_grad * gate * (1.0 + pre * (1.0 - gate))).astype(BF16)
    first.wait()

    def product():
        doc_rows, block = owner_rows(stage[CHUNK:], docs)
        grads = jnp.dot(grad_ref[...], doc_rows, preferred_element_type=F32)
        grads = [jnp.where(block == float(b), grads, 0.0).astype(BF16) for b in range(blocks)]
        return jnp.dot(
            jnp.concatenate(grads, axis=0), stage[:CHUNK], preferred_element_type=F32
        ).reshape(blocks, cols, width)

    @pl.when(chunks <= 1)
    def _():
        out_ref[...] = product().astype(BF16)

    @pl.when(chunks > 1)
    def _():
        total_ref[...] = product()

        @pl.loop(1, chunks)
        def _(chunk):
            later = pltpu.make_async_copy(packed_hbm.at[chunk], stage, sem)
            later.start()
            later.wait()
            total_ref[...] += product()

        out_ref[...] = total_ref[...].astype(BF16)


def backward(count, parts, pre_t, packed, blocks):
    cols, docs = pre_t.shape
    width = packed.shape[2]
    return pl.pallas_call(
        backward_kernel,
        out_shape=jax.ShapeDtypeStruct((blocks, cols, width), BF16),
        in_specs=[SMEM, VMEM, VMEM, HBM],
        out_specs=VMEM,
        scratch_shapes=[
            pltpu.VMEM(packed.shape[1:], BF16),
            pltpu.VMEM((cols, docs), BF16),
            pltpu.VMEM((blocks, cols, width), F32),
            pltpu.SemaphoreType.DMA(()),
        ],
        compiler_params=pltpu.CompilerParams(vmem_limit_bytes=16 << 20),
    )(count, parts, pre_t, packed)


def row_picks(place_ref):
    owners = place_ref.shape[0]
    half = ROWS // 2
    low_rank = iota((half, 1), 0).astype(F32)
    places = [place_ref[o : o + 1] for o in range(owners)]
    low = jnp.concatenate([jnp.where(low_rank == p, 1.0, 0.0) for p in places], axis=0)
    high = jnp.concatenate([jnp.where(low_rank + half == p, 1.0, 0.0) for p in places], axis=0)
    return low.astype(BF16), high.astype(BF16)


def hidden_kernel(parts_ref, place_ref, pre_ref, sent_ref):
    pre = parts_ref[0].astype(F32)
    for shard in range(1, parts_ref.shape[0]):
        pre += parts_ref[shard].astype(F32)
    pre_ref[...] = pre
    hidden = jax.nn.silu(pre).astype(BF16)
    none = jnp.zeros_like(hidden)
    low, high = row_picks(place_ref)
    rows = lax.dot_general(
        low, jnp.concatenate([hidden, none], axis=0), NT, preferred_element_type=F32
    ) + lax.dot_general(
        high, jnp.concatenate([none, hidden], axis=0), NT, preferred_element_type=F32
    )
    sent_ref[...] = rows.astype(BF16).reshape(sent_ref.shape)


def label_kernel(got_ref, weight_ref, pos_ref, neg_ref, back_ref, rows_ref, grad_ref):
    owners, half, lanes = got_ref.shape
    cols = lanes // 2
    first = iota((half, lanes), 1) < cols
    lows, highs = [], []
    for pair in range(owners // 2):
        left = got_ref[2 * pair].astype(F32)
        right = got_ref[2 * pair + 1].astype(F32)
        lows.append(jnp.where(first, left, pltpu.roll(right, cols, 1)))
        highs.append(jnp.where(first, pltpu.roll(left, cols, 1), right))
    rows = jnp.concatenate(
        [jnp.concatenate(lows, axis=1), jnp.concatenate(highs, axis=1)], axis=0
    ).astype(BF16)
    rows_ref[...] = rows
    weight = weight_ref[...]
    logit = lax.dot_general(rows, weight, NT, preferred_element_type=F32)
    sig = jax.nn.sigmoid(logit)
    grad_pos = (sig - 1.0).astype(BF16).astype(F32)
    grad_neg = sig.astype(BF16).astype(F32)
    grad = (pos_ref[...] * grad_pos + neg_ref[...] * grad_neg).astype(BF16)
    grad_ref[...] = grad
    terms = jnp.dot(grad, weight, preferred_element_type=F32)
    for pair in range(owners // 2):
        low = terms[:half, pair * lanes : (pair + 1) * lanes]
        high = terms[half:, pair * lanes : (pair + 1) * lanes]
        back_ref[2 * pair] = jnp.where(first, low, pltpu.roll(high, cols, 1)).astype(BF16)
        back_ref[2 * pair + 1] = jnp.where(first, pltpu.roll(low, cols, 1), high).astype(BF16)


def collect_kernel(came_ref, place_ref, out_ref):
    owners, half, lanes = came_ref.shape
    cols = lanes // 2
    came = came_ref[...].reshape(owners * half, lanes)
    low, high = row_picks(place_ref)
    tn = (((0,), (0,)), ((), ()))
    part = (
        lax.dot_general(came, low, tn, preferred_element_type=F32)[:cols]
        + lax.dot_general(came, high, tn, preferred_element_type=F32)[cols:]
    ).astype(BF16)
    for shard in range(out_ref.shape[0]):
        out_ref[shard] = part


def local_call(kernel, inputs, *shapes):
    return pl.pallas_call(
        kernel,
        out_shape=tuple(jax.ShapeDtypeStruct(shape, kind) for shape, kind in shapes),
        in_specs=[VMEM] * len(inputs),
        out_specs=(VMEM,) * len(shapes),
        compiler_params=pltpu.CompilerParams(vmem_limit_bytes=16 << 20),
    )(*inputs)


def on_device(doc_blocks, doc_counts, doc_values, pos_labels, neg_labels, in_weight, out_weight):
    block_count, block_size, col_count = in_weight.shape
    doc_total, slot_count = doc_blocks.shape
    lab_count, hidden_width = out_weight.shape
    feat_index = lax.axis_index("feat")
    label_index = lax.axis_index("label")
    owners = lax.axis_size("label")
    shards = lax.axis_size("feat")
    half = ROWS // 2

    local_ids = doc_blocks - feat_index * block_count
    slots = jnp.arange(slot_count, dtype=jnp.int32)
    listed = (slots[None, :] < doc_counts[:, None]) & (local_ids >= 0) & (local_ids < block_count)
    groups = doc_total // GROUP
    code = jnp.where(listed, local_ids, -1).reshape(groups, GROUP * slot_count)
    code = jnp.pad(code, ((0, -groups % 8), (0, 0)), constant_values=-1)
    packed, chunks, copies = forward(
        code,
        doc_values.reshape(groups, GROUP * slot_count, block_size),
        jnp.swapaxes(in_weight, 1, 2),
        shards,
    )

    labels_t = jnp.concatenate([pos_labels.T, neg_labels.T], axis=0)
    rel = labels_t // lab_count - feat_index * owners
    count = jnp.sum(
        (rel[None] == jnp.arange(owners, dtype=jnp.int32)[:, None, None]).astype(F32), axis=1
    )
    docs = jnp.arange(doc_total, dtype=jnp.int32)
    before = (docs[:, None] < docs[None, :]).astype(BF16)
    base = jnp.dot(count.astype(BF16), before, preferred_element_type=F32)
    place = jnp.where(count > 0, base, -1.0)
    ranks = jnp.arange(ROWS, dtype=jnp.int32).astype(F32)
    nt = NT
    arrived = lax.all_to_all(copies, "feat", 0, 0, tiled=True)
    row_shape = (owners, half, 2 * col_count)
    pre_t, sent = local_call(
        hidden_kernel, (arrived, place), (copies.shape[1:], F32), (row_shape, BF16)
    )
    got = lax.all_to_all(sent, "label", 0, 0, tiled=True)

    own = labels_t - (feat_index * owners + label_index) * lab_count
    own = jnp.where((own >= 0) & (own < lab_count), own + 1, 0).astype(BF16)
    own_place = lax.dynamic_slice_in_dim(place, label_index, 1, 0)
    own_pick = (own_place == ranks[:, None]).astype(BF16)
    row_labels = lax.dot_general(own_pick, own, nt, preferred_element_type=F32)
    names = jnp.arange(1, lab_count + 1, dtype=jnp.int32).astype(F32)
    hits = (row_labels[:, :, None] == names[None, None, :]).astype(F32)
    pos_slots = pos_labels.shape[1]
    pos_count = jnp.sum(hits[:, :pos_slots], axis=1)
    neg_count = jnp.sum(hits[:, pos_slots:], axis=1)
    back, rows, label_grad = local_call(
        label_kernel,
        (got, out_weight, pos_count, neg_count),
        (row_shape, BF16),
        ((ROWS, hidden_width), BF16),
        ((ROWS, lab_count), BF16),
    )
    came = lax.all_to_all(back, "label", 0, 0, tiled=True)
    (copies,) = local_call(collect_kernel, (came, place), (copies.shape, BF16))
    parts = lax.all_to_all(copies, "feat", 0, 0, tiled=True)
    out_grad = lax.dot_general(
        label_grad, rows, (((0,), (0,)), ((), ())), preferred_element_type=F32
    ).astype(BF16)
    in_grad = backward(chunks, parts, pre_t, packed, block_count)
    return (jnp.swapaxes(in_grad, 1, 2), out_grad)


def solution(mesh):
    placed = (P(), P(), P(), P(), P(), P("feat", None, "label"), P(("feat", "label"), None))
    return jax.shard_map(
        on_device,
        mesh=mesh,
        in_specs=placed,
        out_specs=(P("feat", None, "label"), P(("feat", "label"), None)),
        check_vma=False,
    )
```

time: 121 us -> 105 us (0.87)
  matrix products: 22.5 us -> 1.78 us
  blocking collectives: 0 us -> 20.4 us
  waiting for transfers between devices: 51.4 us -> 36.8 us
  Pallas kernels: 0 us -> 10.9 us
  starting transfers between devices: 36.2 us -> 31.2 us
  local copies, waits for them, and re-layouts: 4.41 us -> 0.92 us
  other arithmetic: 4.79 us -> 1.38 us
    dot_general x9 -> x0, matrix products: 20.8 us -> none  [the longest x1 7.57 us: on_device(): jnp.einsum('hd,dbv->bhv', pre_grad, dense, preferred_element_type=F32)]
    all_to_all x0 -> x1, blocking collectives: none -> 20.4 us  [on_device(): came = lax.all_to_all(back, 'label', 0, 0, tiled=True)]
    all_to_all x3 -> x2, waiting for transfers between devices: 37.1 us -> 21.4 us  [the longest x1 11.4 us: on_device(): parts = lax.all_to_all(copies, 'feat', 0, 0, tiled=True)]
    pallas_call x0 -> x5, Pallas kernels: none -> 10.9 us  [the longest x1 4.94 us: forward(): pl.pallas_call(forward_kernel, out_shape=(jax.ShapeDtypeStruct((most, CHU...]
    all_to_all x3 -> x2, starting transfers between devices: 16.3 us -> 11.3 us  [the longest x1 7.6 us: on_device(): arrived = lax.all_to_all(copies, 'feat', 0, 0, tiled=True)]
    broadcast_in_dim x2 -> x0, local copies, waits for them, and re-layouts: 1.96 us -> none  [spread(): copies = jnp.broadcast_to(part.astype(BF16)[None], (shards,) + part.shape)]
    reshape x6 -> x1, local copies, waits for them, and re-layouts: 1.84 us -> 0.14 us  [on_device(): code = jnp.where(listed, local_ids, -1).reshape(groups, GROUP * slot_count)]
    all_to_all x1, waiting for transfers between devices: 14.2 us -> 15.4 us  [on_device(): got = lax.all_to_all(sent, 'label', 0, 0, tiled=True)]
  transfers between devices with their start and end apart: 4 -> 3, of which waited for: 4 -> 3; matrix products, arithmetic and copies ran while one was open for 3% -> 2% of each run, Pallas kernels for 0% -> 0%
where the time goes in v2:
time: 105 us; the launch traced here: 104 us
  waiting for transfers between devices  36.8 us (35%)
  starting transfers between devices  31.2 us (30%)
  blocking collectives  20.4 us (19%)
  Pallas kernels  10.9 us (10%)
  matrix products  1.78 us (2%)
  other arithmetic  1.38 us (1%)
    all_to_all x1, blocking collectives, on_device(): came = lax.all_to_all(back, 'label', 0, 0, tiled=True)  20.4 us
    all_to_all x1, starting transfers between devices, on_device(): got = lax.all_to_all(sent, 'label', 0, 0, tiled=True)  19.9 us
    all_to_all x1, waiting for transfers between devices, on_device(): got = lax.all_to_all(sent, 'label', 0, 0, tiled=True)  15.4 us
    all_to_all x1, waiting for transfers between devices, on_device(): parts = lax.all_to_all(copies, 'feat', 0, 0, tiled=True)  11.4 us
    all_to_all x1, waiting for transfers between devices, on_device(): arrived = lax.all_to_all(copies, 'feat', 0, 0, tiled=True)  9.98 us
    all_to_all x1, starting transfers between devices, on_device(): arrived = lax.all_to_all(copies, 'feat', 0, 0, tiled=True)  7.6 us
    pallas_call x1, Pallas kernels, forward(): pl.pallas_call(forward_kernel, out_shape=(jax.ShapeDtypeStruct((most, CHU...  4.94 us
    all_to_all x1, starting transfers between devices, on_device(): parts = lax.all_to_all(copies, 'feat', 0, 0, tiled=True)  3.75 us
  transfers between devices with their start and end apart: 3, of which 3 were waited for; matrix products, arithmetic and copies ran while one was open for 2% of the time, Pallas kernels for 0%

profile of v2, /device:TPU:1, one launch (start us, length us, event | category | flops | bytes accessed | tf_op | source)
XLA Modules:
  0.0 104.1 jit_solution(8113262391559892132)
XLA Ops:
  0.6 0.7 fusion.10
  1.4 0.1 copy.11
  1.5 0.1 reshape.87
  1.6 0.6 pad.4.code_hbm
  2.2 4.9 %shard_map.86 = (bf16[12,272,256]{2,1,0:T(8,128)(2,1)}, s32[1,1]{1,0:T(1,128)}, bf16[16,64,384]{2,1,0:T(8,128)(2,1)}) custom-call(s32[16,256]{1,0:T(8,128)} %pad.4.code_hbm, bf16[12,256,256]{2,1,0:T(8,128)(2,1)} %bitcast.7, bf16[32,64,256]{2,1,0:T(8,128)(2,1)} %bitcast.8), custom_call_target="tpu_custom_call" | custom-call | tf_op jit(solution)/shard_map/pallas_call | solution.py:125
  7.2 7.6 %all-to-all-start = ((bf16[16,64,384]{2,1,0:T(8,128)(2,1)}), bf16[16,64,384]{2,1,0:T(8,128)(2,1)S(1)}, u32[]{:S(2)}, u32[]{:S(2)}) async-start(bf16[16,64,384]{2,1,0:T(8,128)(2,1)} %get-tuple-element.11), calls=%async_computation | async-start | bytes 1572864 | tf_op jit(solution)/shard_map/all_to_all | solution.py:320
  14.9 0.2 convert_reduce_fusion
  15.1 0.2 convolution_select_fusion.place_ref
  15.3 0.2 fusion.3
  15.5 10.0 %all-to-all-done.parts_ref = bf16[16,64,384]{2,1,0:T(8,128)(2,1)S(1)} async-done(((bf16[16,64,384]{2,1,0:T(8,128)(2,1)}), bf16[16,64,384]{2,1,0:T(8,128)(2,1)S(1)}, u32[]{:S(2)}, u32[]{:S(2)}) %all-to-all-start) | async-done | bytes 786464 | tf_op jit(solution)/shard_map/all_to_all | solution.py:320
  25.5 1.1 %shard_map.87 = (f32[64,384]{1,0:T(8,128)S(1)}, bf16[32,16,128]{2,1,0:T(8,128)(2,1)}) custom-call(bf16[16,64,384]{2,1,0:T(8,128)(2,1)S(1)} %all-to-all-done.parts_ref, f32[32,384]{1,0:T(8,128)S(1)} %convolution_select_fusion.place_ref), custom_call_target="tpu_custom_call" | custom-call | tf_op jit(solution)/shard_map/pallas_call | solution.py:277
  26.6 19.9 %all-to-all-start.1 = ((bf16[32,16,128]{2,1,0:T(8,128)(2,1)}), bf16[32,16,128]{2,1,0:T(8,128)(2,1)S(1)}, u32[]{:S(2)}, u32[]{:S(2)}) async-start(bf16[32,16,128]{2,1,0:T(8,128)(2,1)} %get-tuple-element.12), calls=%async_computation.1 | async-start | bytes 262144 | tf_op jit(solution)/shard_map/all_to_all | solution.py:325
  46.5 0.2 compare_convert_fusion
  46.7 0.1 slice_reduce_fusion.1.pos_ref
  46.8 0.1 slice_reduce_fusion.neg_ref
  46.9 15.4 %all-to-all-done.1.got_ref = bf16[32,16,128]{2,1,0:T(8,128)(2,1)S(1)} async-done(((bf16[32,16,128]{2,1,0:T(8,128)(2,1)}), bf16[32,16,128]{2,1,0:T(8,128)(2,1)S(1)}, u32[]{:S(2)}, u32[]{:S(2)}) %all-to-all-start.1) | async-done | bytes 131104 | tf_op jit(solution)/shard_map/all_to_all | solution.py:325
  62.3 0.0 copy-done.1
  62.3 1.0 shard_map.88
  63.3 20.4 %all_to_all.20.came_ref = bf16[32,16,128]{2,1,0:T(8,128)(2,1)S(1)} all-to-all(bf16[32,16,128]{2,1,0:T(8,128)(2,1)S(1)} %get-tuple-element.13), channel_id=1, replica_groups=mesh['feat'=16,'label'=32] {'label'}, dimensions={0} | all-to-all | bytes 262144 | tf_op jit(solution)/shard_map/all_to_all | solution.py:344
  83.7 1.3 %shard_map.89 = bf16[16,64,384]{2,1,0:T(8,128)(2,1)} custom-call(bf16[32,16,128]{2,1,0:T(8,128)(2,1)S(1)} %all_to_all.20.came_ref, f32[32,384]{1,0:T(8,128)S(1)} %convolution_select_fusion.place_ref), custom_call_target="tpu_custom_call" | custom-call | tf_op jit(solution)/shard_map/pallas_call | solution.py:277
  85.0 3.7 %all-to-all-start.3 = ((bf16[16,64,384]{2,1,0:T(8,128)(2,1)}), bf16[16,64,384]{2,1,0:T(8,128)(2,1)S(1)}, u32[]{:S(2)}, u32[]{:S(2)}) async-start(bf16[16,64,384]{2,1,0:T(8,128)(2,1)} %shard_map.89), calls=%async_computation.3 | async-start | bytes 1572864 | tf_op jit(solution)/shard_map/all_to_all | solution.py:346
  88.8 1.4 %convolution_convert_fusion = bf16[256,2048]{1,0:T(8,128)(2,1)} fusion(bf16[32,256]{1,0:T(8,128)(2,1)S(1)} %get-tuple-element.16, bf16[32,2048]{1,0:T(8,128)(2,1)S(1)} %get-tuple-element.17), kind=kOutput, calls=%fused_computation | convolution fusion | flops 34078720 | bytes 1196032 | tf_op jit(solution)/shard_map/dot_general | solution.py:347
  90.2 11.4 %all-to-all-done.3.parts_ref = bf16[16,64,384]{2,1,0:T(8,128)(2,1)S(1)} async-done(((bf16[16,64,384]{2,1,0:T(8,128)(2,1)}), bf16[16,64,384]{2,1,0:T(8,128)(2,1)S(1)}, u32[]{:S(2)}, u32[]{:S(2)}) %all-to-all-start.3) | async-done | bytes 786464 | tf_op jit(solution)/shard_map/all_to_all | solution.py:346
  101.6 2.5 %shard_map.90 = bf16[32,64,256]{2,1,0:T(8,128)(2,1)} custom-call(s32[1,1]{1,0:T(1,128)} %get-tuple-element.10.count_ref, bf16[16,64,384]{2,1,0:T(8,128)(2,1)S(1)} %all-to-all-done.3.parts_ref, f32[64,384]{1,0:T(8,128)S(1)} %get-tuple-element.14.pre_ref, bf16[12,272,256]{2,1,0:T(8,128)(2,1)S(1)} %copy-done), custom_call_target="tpu_custom_call" | custom-call | tf_op jit(solution)/shard_map/pallas_call | solution.py:192
  (11 shorter events, 0.1 us)
Async XLA Ops:
  2.2 12.6 %copy-start.2 = (s32[384,24]{0,1:T(8,128)S(1)}, s32[384,24]{0,1:T(8,128)}, u32[]{:S(2)}) copy-start(s32[384,24]{0,1:T(8,128)} %param.11) | copy-start | bytes 110596
  2.2 12.6 %copy-start.3 = (s32[384,8]{0,1:T(8,128)S(1)}, s32[384,8]{0,1:T(8,128)}, u32[]{:S(2)}) copy-start(s32[384,8]{0,1:T(8,128)} %param.10) | copy-start | bytes 36868
  7.2 18.3 %all-to-all-start = ((bf16[16,64,384]{2,1,0:T(8,128)(2,1)}), bf16[16,64,384]{2,1,0:T(8,128)(2,1)S(1)}, u32[]{:S(2)}, u32[]{:S(2)}) async-start(bf16[16,64,384]{2,1,0:T(8,128)(2,1)} %get-tuple-element.11), calls=%async_computation | async-start | bytes 1572864 | tf_op jit(solution)/shard_map/all_to_all | solution.py:320
  15.5 46.8 %copy-start.1 = (bf16[256,2048]{1,0:T(8,128)(2,1)S(1)}, bf16[256,2048]{1,0:T(8,128)(2,1)}, u32[]{:S(2)}) copy-start(bf16[256,2048]{1,0:T(8,128)(2,1)} %weight_ref.1) | copy-start | bytes 3145732
  26.6 35.7 %all-to-all-start.1 = ((bf16[32,16,128]{2,1,0:T(8,128)(2,1)}), bf16[32,16,128]{2,1,0:T(8,128)(2,1)S(1)}, u32[]{:S(2)}, u32[]{:S(2)}) async-start(bf16[32,16,128]{2,1,0:T(8,128)(2,1)} %get-tuple-element.12), calls=%async_computation.1 | async-start | bytes 262144 | tf_op jit(solution)/shard_map/all_to_all | solution.py:325
  85.0 16.6 %copy-start = (bf16[12,272,256]{2,1,0:T(8,128)(2,1)S(1)}, bf16[12,272,256]{2,1,0:T(8,128)(2,1)}, u32[]{:S(2)}) copy-start(bf16[12,272,256]{2,1,0:T(8,128)(2,1)} %get-tuple-element.15.packed_hbm) | copy-start | bytes 5013508
  85.0 16.6 %all-to-all-start.3 = ((bf16[16,64,384]{2,1,0:T(8,128)(2,1)}), bf16[16,64,384]{2,1,0:T(8,128)(2,1)S(1)}, u32[]{:S(2)}, u32[]{:S(2)}) async-start(bf16[16,64,384]{2,1,0:T(8,128)(2,1)} %shard_map.89), calls=%async_computation.3 | async-start | bytes 1572864 | tf_op jit(solution)/shard_map/all_to_all | solution.py:346

commit v3 on v2

--- a/solution.py
+++ b/solution.py
@@ -7,12 +7,14 @@
 
 F32 = jnp.float32
 BF16 = jnp.bfloat16
-ROWS = 32
+PAIRS = 24
+QUARTER = 4
 
 
 GROUP = 32
 CHUNK = 256
 NOTES = 16
+PIECES = 4
 VMEM = pl.BlockSpec(memory_space=pltpu.VMEM)
 SMEM = pl.BlockSpec(memory_space=pltpu.SMEM)
 HBM = pl.BlockSpec(memory_space=pltpu.HBM)
@@ -34,14 +36,19 @@
 
 
 def forward_kernel(
-    code_hbm, values_hbm, weight_hbm, packed_hbm, count_ref, out_ref,
-    code_ref, values, weight, rank_ref, stage, total_ref, sems, weight_sem, stage_sem,
+    ids_hbm, used_hbm, values_hbm, weight_hbm, packed_hbm, count_ref, out_ref,
+    ids_ref, used_ref, code_ref, values, weight, rank_ref, stage, total_ref,
+    sems, weight_sem, stage_sem, id_sems,
 ):
     groups = values.shape[0]
     blocks, cols, width = weight.shape
     docs = groups * GROUP
-    code_load = pltpu.make_async_copy(code_hbm, code_ref, stage_sem)
-    code_load.start()
+    id_loads = [
+        pltpu.make_async_copy(ids_hbm, ids_ref, id_sems.at[0]),
+        pltpu.make_async_copy(used_hbm, used_ref, id_sems.at[1]),
+    ]
+    for load in id_loads:
+        load.start()
     loads = [
         pltpu.make_async_copy(values_hbm.at[g], values.at[g], sems.at[g]) for g in range(groups)
     ]
@@ -50,9 +57,22 @@
     weight_load = pltpu.make_async_copy(weight_hbm, weight, weight_sem)
     weight_load.start()
 
-    code_load.wait()
-    code = code_ref[...].astype(F32)
-    pad_groups, lanes = code.shape
+    for load in id_loads:
+        load.wait()
+    slots, _ = ids_ref.shape
+    lanes = GROUP * slots
+    local = ids_ref[...] - lax.axis_index("feat") * blocks
+    inside = (local >= 0) & (local < blocks) & (iota((slots, 1), 0) < used_ref[...])
+    ids = jnp.where(inside, local, -1).astype(F32)
+    ids = jnp.concatenate([ids[:, g * GROUP : (g + 1) * GROUP] for g in range(groups)], axis=0)
+    spread = one_hot(iota((GROUP, lanes), 0), iota((GROUP, lanes), 1) // slots)
+    wide = jnp.dot(ids.astype(BF16), spread, preferred_element_type=F32)
+    own_slot = iota(wide.shape, 0) % slots == iota(wide.shape, 1) % slots
+    wide = jnp.where(own_slot, wide, 0.0).reshape(groups, slots, lanes)
+    pad_groups = code_ref.shape[0]
+    code_ref[...] = jnp.full(code_ref.shape, -1.0, F32)
+    code_ref[:groups] = jnp.sum(wide, axis=1)
+    code = code_ref[...]
     listed = jnp.where(code >= 0.0, 1.0, 0.0)
     listed16 = listed.astype(BF16)
     ahead = jnp.where(iota((lanes, lanes), 0) < iota((lanes, lanes), 1), 1.0, 0.0).astype(BF16)
@@ -76,7 +96,7 @@
         notes = jnp.zeros((NOTES, CHUNK), F32)
         for g in range(groups):
             pick = one_hot(spots, rank_ref[g : g + 1])
-            told = jnp.where(note_row == 0, code_ref[g : g + 1].astype(F32), 0.0)
+            told = jnp.where(note_row == 0, code_ref[g : g + 1], 0.0)
             told = jnp.where(note_row == 1, lane_doc, told)
             told = jnp.where(note_row == 2, float(g), told).astype(BF16)
             notes += lax.dot_general(told, pick, NT, preferred_element_type=F32)
@@ -117,11 +137,12 @@
         out_ref[shard] = part
 
 
-def forward(code, values, weight_t, shards):
+def forward(ids, used, values, weight_t, shards):
     blocks, cols, width = weight_t.shape
     groups, lanes, _ = values.shape
     docs = groups * GROUP
     most = -(-groups * lanes // CHUNK)
+    code_shape = (-(-groups // 8) * 8, lanes)
     return pl.pallas_call(
         forward_kernel,
         out_shape=(
@@ -129,25 +150,30 @@
             jax.ShapeDtypeStruct((1, 1), jnp.int32),
             jax.ShapeDtypeStruct((shards, cols, docs), BF16),
         ),
-        in_specs=[HBM, HBM, HBM],
+        in_specs=[HBM] * 4,
         out_specs=(HBM, SMEM, VMEM),
         scratch_shapes=[
-            pltpu.VMEM(code.shape, jnp.int32),
+            pltpu.VMEM(ids.shape, jnp.int32),
+            pltpu.VMEM(used.shape, jnp.int32),
+            pltpu.VMEM(code_shape, F32),
             pltpu.VMEM(values.shape, BF16),
             pltpu.VMEM(weight_t.shape, BF16),
-            pltpu.VMEM(code.shape, F32),
+            pltpu.VMEM(code_shape, F32),
             pltpu.VMEM((CHUNK + NOTES, width), BF16),
             pltpu.VMEM((cols, docs), F32),
             pltpu.SemaphoreType.DMA((groups,)),
             pltpu.SemaphoreType.DMA(()),
             pltpu.SemaphoreType.DMA(()),
+            pltpu.SemaphoreType.DMA((2,)),
         ],
         compiler_params=pltpu.CompilerParams(vmem_limit_bytes=60 << 20),
-    )(code, values, weight_t)
-
-
-def backward_kernel(count_ref, parts_ref, pre_ref, packed_hbm, out_ref, stage, grad_ref, total_ref, sem):
-    blocks, cols, width = out_ref.shape
+    )(ids, used, values, weight_t)
+
+
+def backward_kernel(
+    count_ref, parts_ref, pre_ref, packed_hbm, out_hbm, stage, grad_ref, total_ref, held, sem, sems
+):
+    blocks, cols, width = held.shape
     docs = pre_ref.shape[1]
     chunks = count_ref[0, 0]
     first = pltpu.make_async_copy(packed_hbm.at[0], stage, sem)
@@ -159,31 +185,50 @@
     gate = jax.nn.sigmoid(pre)
     grad_ref[...] = (hidden_grad * gate * (1.0 + pre * (1.0 - gate))).astype(BF16)
     first.wait()
-
-    def product():
+    step = blocks // PIECES
+
+    def slot_grads():
         doc_rows, block = owner_rows(stage[CHUNK:], docs)
-        grads = jnp.dot(grad_ref[...], doc_rows, preferred_element_type=F32)
-        grads = [jnp.where(block == float(b), grads, 0.0).astype(BF16) for b in range(blocks)]
+        return jnp.dot(grad_ref[...], doc_rows, preferred_element_type=F32), block
+
+    def product(grads, block, piece):
+        own = [
+            jnp.where(block == float(b), grads, 0.0).astype(BF16)
+            for b in range(piece * step, (piece + 1) * step)
+        ]
         return jnp.dot(
-            jnp.concatenate(grads, axis=0), stage[:CHUNK], preferred_element_type=F32
-        ).reshape(blocks, cols, width)
+            jnp.concatenate(own, axis=0), stage[:CHUNK], preferred_element_type=F32
+        ).reshape(step, cols, width)
+
+    def finish(piece_of):
+        saves = []
+        for piece in range(PIECES):
+            part = pl.ds(piece * step, step)
+            held[part] = piece_of(piece).astype(BF16)
+            saves.append(pltpu.make_async_copy(held.at[part], out_hbm.at[part], sems.at[piece]))
+            saves[-1].start()
+        for save in saves:
+            save.wait()
 
     @pl.when(chunks <= 1)
     def _():
-        out_ref[...] = product().astype(BF16)
+        grads, block = slot_grads()
+        finish(lambda piece: product(grads, block, piece))
 
     @pl.when(chunks > 1)
     def _():
-        total_ref[...] = product()
-
-        @pl.loop(1, chunks)
+        total_ref[...] = jnp.zeros_like(total_ref)
+
+        @pl.loop(0, chunks)
         def _(chunk):
             later = pltpu.make_async_copy(packed_hbm.at[chunk], stage, sem)
             later.start()
             later.wait()
-            total_ref[...] += product()
-
-        out_ref[...] = total_ref[...].astype(BF16)
+            grads, block = slot_grads()
+            for piece in range(PIECES):
+                total_ref[pl.ds(piece * step, step)] += product(grads, block, piece)
+
+        finish(lambda piece: total_ref[pl.ds(piece * step, step)])
 
 
 def backward(count, parts, pre_t, packed, blocks):
@@ -193,25 +238,65 @@
         backward_kernel,
         out_shape=jax.ShapeDtypeStruct((blocks, cols, width), BF16),
         in_specs=[SMEM, VMEM, VMEM, HBM],
-        out_specs=VMEM,
+        out_specs=HBM,
         scratch_shapes=[
             pltpu.VMEM(packed.shape[1:], BF16),
             pltpu.VMEM((cols, docs), BF16),
             pltpu.VMEM((blocks, cols, width), F32),
+            pltpu.VMEM((blocks, cols, width), BF16),
             pltpu.SemaphoreType.DMA(()),
+            pltpu.SemaphoreType.DMA((PIECES,)),
         ],
         compiler_params=pltpu.CompilerParams(vmem_limit_bytes=16 << 20),
     )(count, parts, pre_t, packed)
 
 
 def row_picks(place_ref):
-    owners = place_ref.shape[0]
-    half = ROWS // 2
-    low_rank = iota((half, 1), 0).astype(F32)
-    places = [place_ref[o : o + 1] for o in range(owners)]
-    low = jnp.concatenate([jnp.where(low_rank == p, 1.0, 0.0) for p in places], axis=0)
-    high = jnp.concatenate([jnp.where(low_rank + half == p, 1.0, 0.0) for p in places], axis=0)
-    return low.astype(BF16), high.astype(BF16)
+    owners, docs = place_ref.shape
+    tile = 2 * QUARTER
+    within = iota((tile, 1), 0)
+    first = within < QUARTER
+    rank = (within % QUARTER).astype(F32)
+    places = [
+        jnp.where(first, place_ref[o : o + 1], place_ref[o + 1 : o + 2]) for o in range(0, owners, 2)
+    ]
+    picks = []
+    for start in (0, PAIRS // 2):
+        picks.append(
+            jnp.concatenate(
+                [
+                    jnp.where(p == rank + float(start + offset), 1.0, 0.0)
+                    for offset in range(0, PAIRS // 2, QUARTER)
+                    for p in places
+                ],
+                axis=0,
+            ).astype(BF16)
+        )
+    return picks
+
+
+def read_rows(ref):
+    owners, _, lanes = ref.shape
+    return [
+        [
+            jnp.concatenate(
+                [ref[o + i, :, at : at + 128].astype(F32) for i in range(2)], axis=0
+            )
+            for o in range(0, owners, 2)
+        ]
+        for at in range(0, lanes, 128)
+    ]
+
+
+def write_rows(ref, group, pair, tile):
+    at = group * 128
+    ref[2 * pair, :, at : at + 128] = tile[:QUARTER].astype(BF16)
+    ref[2 * pair + 1, :, at : at + 128] = tile[QUARTER:].astype(BF16)
+
+
+def swap(tile):
+    keep = (iota(tile.shape, 0) < QUARTER) == (iota(tile.shape, 1) < 64)
+    return jnp.where(keep, tile, pltpu.roll(pltpu.roll(tile, QUARTER, 0), 64, 1))
 
 
 def hidden_kernel(parts_ref, place_ref, pre_ref, sent_ref):
@@ -227,22 +312,15 @@
     ) + lax.dot_general(
         high, jnp.concatenate([none, hidden], axis=0), NT, preferred_element_type=F32
     )
-    sent_ref[...] = rows.astype(BF16).reshape(sent_ref.shape)
+    pairs = sent_ref.shape[0] // 2
+    for index in range(rows.shape[0] // 8):
+        write_rows(sent_ref, index // pairs, index % pairs, rows[index * 8 : (index + 1) * 8])
 
 
 def label_kernel(got_ref, weight_ref, pos_ref, neg_ref, back_ref, rows_ref, grad_ref):
-    owners, half, lanes = got_ref.shape
-    cols = lanes // 2
-    first = iota((half, lanes), 1) < cols
-    lows, highs = [], []
-    for pair in range(owners // 2):
-        left = got_ref[2 * pair].astype(F32)
-        right = got_ref[2 * pair + 1].astype(F32)
-        lows.append(jnp.where(first, left, pltpu.roll(right, cols, 1)))
-        highs.append(jnp.where(first, pltpu.roll(left, cols, 1), right))
-    rows = jnp.concatenate(
-        [jnp.concatenate(lows, axis=1), jnp.concatenate(highs, axis=1)], axis=0
-    ).astype(BF16)
+    groups = [jnp.concatenate([swap(t) for t in tiles], axis=1) for tiles in read_rows(got_ref)]
+    groups.append(jnp.zeros_like(groups[0]))
+    rows = jnp.concatenate(groups, axis=0).astype(BF16)
     rows_ref[...] = rows
     weight = weight_ref[...]
     logit = lax.dot_general(rows, weight, NT, preferred_element_type=F32)
@@ -252,17 +330,15 @@
     grad = (pos_ref[...] * grad_pos + neg_ref[...] * grad_neg).astype(BF16)
     grad_ref[...] = grad
     terms = jnp.dot(grad, weight, preferred_element_type=F32)
-    for pair in range(owners // 2):
-        low = terms[:half, pair * lanes : (pair + 1) * lanes]
-        high = terms[half:, pair * lanes : (pair + 1) * lanes]
-        back_ref[2 * pair] = jnp.where(first, low, pltpu.roll(high, cols, 1)).astype(BF16)
-        back_ref[2 * pair + 1] = jnp.where(first, pltpu.roll(low, cols, 1), high).astype(BF16)
+    for group in range(PAIRS // 8):
+        for pair in range(back_ref.shape[0] // 2):
+            tile = terms[group * 8 : (group + 1) * 8, pair * 128 : (pair + 1) * 128]
+            write_rows(back_ref, group, pair, swap(tile))
 
 
 def collect_kernel(came_ref, place_ref, out_ref):
-    owners, half, lanes = came_ref.shape
-    cols = lanes // 2
-    came = came_ref[...].reshape(owners * half, lanes)
+    came = jnp.concatenate([t for tiles in read_rows(came_ref) for t in tiles], axis=0).astype(BF16)
+    cols = out_ref.shape[1]
     low, high = row_picks(place_ref)
     tn = (((0,), (0,)), ((), ()))
     part = (
@@ -291,16 +367,11 @@
     label_index = lax.axis_index("label")
     owners = lax.axis_size("label")
     shards = lax.axis_size("feat")
-    half = ROWS // 2
-
-    local_ids = doc_blocks - feat_index * block_count
-    slots = jnp.arange(slot_count, dtype=jnp.int32)
-    listed = (slots[None, :] < doc_counts[:, None]) & (local_ids >= 0) & (local_ids < block_count)
+
     groups = doc_total // GROUP
-    code = jnp.where(listed, local_ids, -1).reshape(groups, GROUP * slot_count)
-    code = jnp.pad(code, ((0, -groups % 8), (0, 0)), constant_values=-1)
     packed, chunks, copies = forward(
-        code,
+        doc_blocks.T,
+        doc_counts.reshape(1, doc_total),
         doc_values.reshape(groups, GROUP * slot_count, block_size),
         jnp.swapaxes(in_weight, 1, 2),
         shards,
@@ -315,10 +386,12 @@
     before = (docs[:, None] < docs[None, :]).astype(BF16)
     base = jnp.dot(count.astype(BF16), before, preferred_element_type=F32)
     place = jnp.where(count > 0, base, -1.0)
-    ranks = jnp.arange(ROWS, dtype=jnp.int32).astype(F32)
+    spot = jnp.arange(PAIRS + 8, dtype=jnp.int32)
+    ranks = spot // 8 * QUARTER + spot % QUARTER + spot % 8 // QUARTER * (PAIRS // 2)
+    ranks = jnp.where(spot < PAIRS, ranks, -2).astype(F32)
     nt = NT
     arrived = lax.all_to_all(copies, "feat", 0, 0, tiled=True)
-    row_shape = (owners, half, 2 * col_count)
+    row_shape = (owners, QUARTER, PAIRS * col_count // QUARTER)
     pre_t, sent = local_call(
         hidden_kernel, (arrived, place), (copies.shape[1:], F32), (row_shape, BF16)
     )
@@ -338,8 +411,8 @@
         label_kernel,
         (got, out_weight, pos_count, neg_count),
         (row_shape, BF16),
-        ((ROWS, hidden_width), BF16),
-        ((ROWS, lab_count), BF16),
+        ((PAIRS + 8, hidden_width), BF16),
+        ((PAIRS + 8, lab_count), BF16),
     )
     came = lax.all_to_all(back, "label", 0, 0, tiled=True)
     (copies,) = local_call(collect_kernel, (came, place), (copies.shape, BF16))

time: 105 us -> 101 us (0.962)
  blocking collectives: 20.4 us -> 18.3 us
  waiting for transfers between devices: 36.8 us -> 35.2 us
    all_to_all x1, blocking collectives: 20.4 us -> 18.3 us  [on_device(): came = lax.all_to_all(back, 'label', 0, 0, tiled=True)]
    all_to_all x1, waiting for transfers between devices: 15.4 us -> 14.2 us  [on_device(): got = lax.all_to_all(sent, 'label', 0, 0, tiled=True)]
    reshape x1, local copies, waits for them, and re-layouts: 0.14 us -> 1.25 us  [on_device(): doc_counts.reshape(1, doc_total)]
where the time goes in v3:
time: 101 us; the launch traced here: 100 us
  waiting for transfers between devices  35.2 us (35%)
  starting transfers between devices  31.2 us (31%)
  blocking collectives  18.3 us (18%)
  Pallas kernels  10.9 us (11%)
  matrix products  1.78 us (2%)
  local copies, waits for them, and re-layouts  1.29 us (1%)
    all_to_all x1, starting transfers between devices, on_device(): got = lax.all_to_all(sent, 'label', 0, 0, tiled=True)  19.8 us
    all_to_all x1, blocking collectives, on_device(): came = lax.all_to_all(back, 'label', 0, 0, tiled=True)  18.3 us
    all_to_all x1, waiting for transfers between devices, on_device(): got = lax.all_to_all(sent, 'label', 0, 0, tiled=True)  14.2 us
    all_to_all x1, waiting for transfers between devices, on_device(): parts = lax.all_to_all(copies, 'feat', 0, 0, tiled=True)  11 us
    all_to_all x1, waiting for transfers between devices, on_device(): arrived = lax.all_to_all(copies, 'feat', 0, 0, tiled=True)  9.98 us
    all_to_all x1, starting transfers between devices, on_device(): arrived = lax.all_to_all(copies, 'feat', 0, 0, tiled=True)  7.6 us
    pallas_call x1, Pallas kernels, forward(): pl.pallas_call(forward_kernel, out_shape=(jax.ShapeDtypeStruct((most, CHU...  5.16 us
    all_to_all x1, starting transfers between devices, on_device(): parts = lax.all_to_all(copies, 'feat', 0, 0, tiled=True)  3.75 us
  transfers between devices with their start and end apart: 3, of which 3 were waited for; matrix products, arithmetic and copies ran while one was open for 2% of the time, Pallas kernels for 0%

profile of v3, /device:TPU:1, one launch (start us, length us, event | category | flops | bytes accessed | tf_op | source)
XLA Modules:
  0.0 100.0 jit_solution(9053398493537099655)
XLA Ops:
  0.6 1.2 %reshape.132.used_hbm = s32[1,384]{1,0:T(1,128)} reshape(s32[384]{0:T(512)} %param.8) | data formatting | bytes 3072 | tf_op jit(solution)/shard_map/reshape | solution.py:374
  1.9 5.2 %shard_map.86 = (bf16[12,272,256]{2,1,0:T(8,128)(2,1)}, s32[1,1]{1,0:T(1,128)}, bf16[16,64,384]{2,1,0:T(8,128)(2,1)}) custom-call(s32[8,384]{1,0:T(8,128)} %bitcast.13, s32[1,384]{1,0:T(1,128)} %reshape.132.used_hbm, bf16[12,256,256]{2,1,0:T(8,128)(2,1)} %bitcast.8, bf16[32,64,256]{2,1,0:T(8,128)(2,1)} %bitcast.9), custom_call_target="tpu_custom_call" | custom-call | tf_op jit(solution)/shard_map/pallas_call | solution.py:146
  7.0 7.6 %all-to-all-start = ((bf16[16,64,384]{2,1,0:T(8,128)(2,1)}), bf16[16,64,384]{2,1,0:T(8,128)(2,1)S(1)}, u32[]{:S(2)}, u32[]{:S(2)}) async-start(bf16[16,64,384]{2,1,0:T(8,128)(2,1)} %get-tuple-element.11), calls=%async_computation | async-start | bytes 1572864 | tf_op jit(solution)/shard_map/all_to_all | solution.py:393
  14.7 0.0 copy-done.2
  14.7 0.0 copy-done.3
  14.7 0.2 convert_reduce_fusion
  15.0 0.2 convolution_select_fusion.place_ref
  15.2 0.2 fusion.3
  15.4 10.0 %all-to-all-done.parts_ref = bf16[16,64,384]{2,1,0:T(8,128)(2,1)S(1)} async-done(((bf16[16,64,384]{2,1,0:T(8,128)(2,1)}), bf16[16,64,384]{2,1,0:T(8,128)(2,1)S(1)}, u32[]{:S(2)}, u32[]{:S(2)}) %all-to-all-start) | async-done | bytes 786464 | tf_op jit(solution)/shard_map/all_to_all | solution.py:393
  25.4 1.1 %shard_map.87 = (f32[64,384]{1,0:T(8,128)S(1)}, bf16[32,4,384]{2,1,0:T(4,128)(2,1)}) custom-call(bf16[16,64,384]{2,1,0:T(8,128)(2,1)S(1)} %all-to-all-done.parts_ref, f32[32,384]{1,0:T(8,128)S(1)} %convolution_select_fusion.place_ref), custom_call_target="tpu_custom_call" | custom-call | tf_op jit(solution)/shard_map/pallas_call | solution.py:353
  26.4 19.8 %all-to-all-start.1 = ((bf16[32,4,384]{2,1,0:T(4,128)(2,1)}), bf16[32,4,384]{2,1,0:T(4,128)(2,1)S(1)}, u32[]{:S(2)}, u32[]{:S(2)}) async-start(bf16[32,4,384]{2,1,0:T(4,128)(2,1)} %get-tuple-element.12), calls=%async_computation.1 | async-start | bytes 196608 | tf_op jit(solution)/shard_map/all_to_all | solution.py:398
  46.3 0.2 compare_convert_fusion
  46.5 0.1 slice_reduce_fusion.1.pos_ref
  46.5 0.1 slice_reduce_fusion.neg_ref
  46.7 14.2 %all-to-all-done.1.got_ref = bf16[32,4,384]{2,1,0:T(4,128)(2,1)S(1)} async-done(((bf16[32,4,384]{2,1,0:T(4,128)(2,1)}), bf16[32,4,384]{2,1,0:T(4,128)(2,1)S(1)}, u32[]{:S(2)}, u32[]{:S(2)}) %all-to-all-start.1) | async-done | bytes 98336 | tf_op jit(solution)/shard_map/all_to_all | solution.py:398
  60.9 0.0 copy-done.1
  60.9 1.0 shard_map.88
  61.8 18.3 %all_to_all.20.came_ref = bf16[32,4,384]{2,1,0:T(4,128)(2,1)S(1)} all-to-all(bf16[32,4,384]{2,1,0:T(4,128)(2,1)S(1)} %get-tuple-element.13), channel_id=1, replica_groups=mesh['feat'=16,'label'=32] {'label'}, dimensions={0} | all-to-all | bytes 196608 | tf_op jit(solution)/shard_map/all_to_all | solution.py:417
  80.2 1.3 %shard_map.89 = bf16[16,64,384]{2,1,0:T(8,128)(2,1)} custom-call(bf16[32,4,384]{2,1,0:T(4,128)(2,1)S(1)} %all_to_all.20.came_ref, f32[32,384]{1,0:T(8,128)S(1)} %convolution_select_fusion.place_ref), custom_call_target="tpu_custom_call" | custom-call | tf_op jit(solution)/shard_map/pallas_call | solution.py:353
  81.5 3.7 %all-to-all-start.3 = ((bf16[16,64,384]{2,1,0:T(8,128)(2,1)}), bf16[16,64,384]{2,1,0:T(8,128)(2,1)S(1)}, u32[]{:S(2)}, u32[]{:S(2)}) async-start(bf16[16,64,384]{2,1,0:T(8,128)(2,1)} %shard_map.89), calls=%async_computation.3 | async-start | bytes 1572864 | tf_op jit(solution)/shard_map/all_to_all | solution.py:419
  85.2 1.4 %convolution_convert_fusion = bf16[256,2048]{1,0:T(8,128)(2,1)} fusion(bf16[32,256]{1,0:T(8,128)(2,1)S(1)} %get-tuple-element.16, bf16[32,2048]{1,0:T(8,128)(2,1)S(1)} %get-tuple-element.17), kind=kOutput, calls=%fused_computation | convolution fusion | flops 34078720 | bytes 1196032 | tf_op jit(solution)/shard_map/dot_general | solution.py:420
  86.6 11.0 %all-to-all-done.3.parts_ref = bf16[16,64,384]{2,1,0:T(8,128)(2,1)S(1)} async-done(((bf16[16,64,384]{2,1,0:T(8,128)(2,1)}), bf16[16,64,384]{2,1,0:T(8,128)(2,1)S(1)}, u32[]{:S(2)}, u32[]{:S(2)}) %all-to-all-start.3) | async-done | bytes 786464 | tf_op jit(solution)/shard_map/all_to_all | solution.py:419
  97.6 0.0 copy-done
  97.6 2.4 %shard_map.90 = bf16[32,64,256]{2,1,0:T(8,128)(2,1)} custom-call(s32[1,1]{1,0:T(1,128)} %get-tuple-element.10.count_ref, bf16[16,64,384]{2,1,0:T(8,128)(2,1)S(1)} %all-to-all-done.3.parts_ref, f32[64,384]{1,0:T(8,128)S(1)} %get-tuple-element.14.pre_ref, bf16[12,272,256]{2,1,0:T(8,128)(2,1)S(1)} %copy-done), custom_call_target="tpu_custom_call" | custom-call | tf_op jit(solution)/shard_map/pallas_call | solution.py:237
  (8 shorter events, 0.1 us)
Async XLA Ops:
  1.9 12.8 %copy-start.2 = (s32[384,24]{0,1:T(8,128)S(1)}, s32[384,24]{0,1:T(8,128)}, u32[]{:S(2)}) copy-start(s32[384,24]{0,1:T(8,128)} %param.11) | copy-start | bytes 110596
  1.9 12.8 %copy-start.3 = (s32[384,8]{0,1:T(8,128)S(1)}, s32[384,8]{0,1:T(8,128)}, u32[]{:S(2)}) copy-start(s32[384,8]{0,1:T(8,128)} %param.10) | copy-start | bytes 36868
  7.0 18.3 %all-to-all-start = ((bf16[16,64,384]{2,1,0:T(8,128)(2,1)}), bf16[16,64,384]{2,1,0:T(8,128)(2,1)S(1)}, u32[]{:S(2)}, u32[]{:S(2)}) async-start(bf16[16,64,384]{2,1,0:T(8,128)(2,1)} %get-tuple-element.11), calls=%async_computation | async-start | bytes 1572864 | tf_op jit(solution)/shard_map/all_to_all | solution.py:393
  15.4 45.5 %copy-start.1 = (bf16[256,2048]{1,0:T(8,128)(2,1)S(1)}, bf16[256,2048]{1,0:T(8,128)(2,1)}, u32[]{:S(2)}) copy-start(bf16[256,2048]{1,0:T(8,128)(2,1)} %weight_ref.1) | copy-start | bytes 3145732
  26.4 34.4 %all-to-all-start.1 = ((bf16[32,4,384]{2,1,0:T(4,128)(2,1)}), bf16[32,4,384]{2,1,0:T(4,128)(2,1)S(1)}, u32[]{:S(2)}, u32[]{:S(2)}) async-start(bf16[32,4,384]{2,1,0:T(4,128)(2,1)} %get-tuple-element.12), calls=%async_computation.1 | async-start | bytes 196608 | tf_op jit(solution)/shard_map/all_to_all | solution.py:398
  81.5 16.2 %copy-start = (bf16[12,272,256]{2,1,0:T(8,128)(2,1)S(1)}, bf16[12,272,256]{2,1,0:T(8,128)(2,1)}, u32[]{:S(2)}) copy-start(bf16[12,272,256]{2,1,0:T(8,128)(2,1)} %get-tuple-element.15.packed_hbm) | copy-start | bytes 5013508
  81.5 16.2 %all-to-all-start.3 = ((bf16[16,64,384]{2,1,0:T(8,128)(2,1)}), bf16[16,64,384]{2,1,0:T(8,128)(2,1)S(1)}, u32[]{:S(2)}, u32[]{:S(2)}) async-start(bf16[16,64,384]{2,1,0:T(8,128)(2,1)} %shard_map.89), calls=%async_computation.3 | async-start | bytes 1572864 | tf_op jit(solution)/shard_map/all_to_all | solution.py:419

commit v4 on v3

--- a/solution.py
+++ b/solution.py
@@ -1,3 +1,5 @@
+import functools
+
 import jax
 import jax.numpy as jnp
 from jax import lax
@@ -35,10 +37,40 @@
     return one_hot(iota((docs, 1), 0).astype(F32), doc), held[0:1]
 
 
+def name_rows(pos_ids, neg_ids, owners, labels, base_ref, pairs_ref, pos_ref, neg_ref):
+    pos_slots, docs = pos_ids.shape
+    ids = jnp.concatenate([pos_ids, neg_ids], axis=0)
+    owner = ids // labels - lax.axis_index("feat") * owners
+    row = iota((owners, 1), 0)
+    count = jnp.zeros((owners, docs), F32)
+    for slot in range(ids.shape[0]):
+        count += jnp.where(owner[slot : slot + 1] == row, 1.0, 0.0)
+    before = jnp.where(iota((docs, docs), 0) < iota((docs, docs), 1), 1.0, 0.0).astype(BF16)
+    base = jnp.dot(count.astype(BF16), before, preferred_element_type=F32)
+    place = jnp.where(count > 0.0, base, -1.0)
+    base_ref[...] = base
+    pairs_ref[...] = count
+
+    me = lax.axis_index("label")
+    own_place = jnp.sum(jnp.where(row == me, place, 0.0), axis=0, keepdims=True)
+    name = jnp.where(owner == me, ids % labels + 1, 0).astype(F32).astype(BF16)
+    spot = iota((PAIRS + 8, 1), 0)
+    rank = spot // 8 * QUARTER + spot % QUARTER + spot % 8 // QUARTER * (PAIRS // 2)
+    rank = jnp.where(spot < PAIRS, rank, -2).astype(F32)
+    listed = lax.dot_general(one_hot(rank, own_place), name, NT, preferred_element_type=F32)
+    names = (iota((1, labels), 1) + 1).astype(F32)
+    hits = [
+        jnp.where(listed[:, slot : slot + 1] == names, 1.0, 0.0) for slot in range(ids.shape[0])
+    ]
+    pos_ref[...] = sum(hits[1:pos_slots], hits[0])
+    neg_ref[...] = sum(hits[pos_slots + 1 :], hits[pos_slots])
+
+
 def forward_kernel(
-    ids_hbm, used_hbm, values_hbm, weight_hbm, packed_hbm, count_ref, out_ref,
-    ids_ref, used_ref, code_ref, values, weight, rank_ref, stage, total_ref,
-    sems, weight_sem, stage_sem, id_sems,
+    ids_hbm, used_hbm, pos_hbm, neg_hbm, values_hbm, weight_hbm,
+    packed_hbm, count_ref, out_ref, base_ref, pairs_ref, pos_ref, neg_ref,
+    ids_ref, used_ref, pos_ids, neg_ids, code_ref, values, weight, rank_ref, stage, total_ref,
+    sems, weight_sem, stage_sem, id_sems, *, owners, labels,
 ):
     groups = values.shape[0]
     blocks, cols, width = weight.shape
@@ -46,6 +78,8 @@
     id_loads = [
         pltpu.make_async_copy(ids_hbm, ids_ref, id_sems.at[0]),
         pltpu.make_async_copy(used_hbm, used_ref, id_sems.at[1]),
+        pltpu.make_async_copy(pos_hbm, pos_ids, id_sems.at[2]),
+        pltpu.make_async_copy(neg_hbm, neg_ids, id_sems.at[3]),
     ]
     for load in id_loads:
         load.start()
@@ -62,7 +96,7 @@
     slots, _ = ids_ref.shape
     lanes = GROUP * slots
     local = ids_ref[...] - lax.axis_index("feat") * blocks
-    inside = (local >= 0) & (local < blocks) & (iota((slots, 1), 0) < used_ref[...])
+    inside = (local >= 0) & (local < blocks) & (iota((slots, 1), 0) < used_ref[...].reshape(1, docs))
     ids = jnp.where(inside, local, -1).astype(F32)
     ids = jnp.concatenate([ids[:, g * GROUP : (g + 1) * GROUP] for g in range(groups)], axis=0)
     spread = one_hot(iota((GROUP, lanes), 0), iota((GROUP, lanes), 1) // slots)
@@ -87,6 +121,9 @@
     count = jnp.sum(listed).astype(jnp.int32)
     chunks = jnp.maximum((count + CHUNK - 1) // CHUNK, 1)
     count_ref[0, 0] = chunks
+    name_rows(
+        pos_ids[...], neg_ids[...], owners, labels, base_ref, pairs_ref, pos_ref, neg_ref
+    )
     note_row = iota((NOTES, lanes), 0)
     lane_doc = (iota((NOTES, lanes), 1) // (lanes // GROUP)).astype(F32)
 
@@ -137,24 +174,30 @@
         out_ref[shard] = part
 
 
-def forward(ids, used, values, weight_t, shards):
+def forward(ids, used, pos, neg, values, weight_t, shards, owners, labels):
     blocks, cols, width = weight_t.shape
     groups, lanes, _ = values.shape
     docs = groups * GROUP
     most = -(-groups * lanes // CHUNK)
     code_shape = (-(-groups // 8) * 8, lanes)
     return pl.pallas_call(
-        forward_kernel,
+        functools.partial(forward_kernel, owners=owners, labels=labels),
         out_shape=(
             jax.ShapeDtypeStruct((most, CHUNK + NOTES, width), BF16),
             jax.ShapeDtypeStruct((1, 1), jnp.int32),
             jax.ShapeDtypeStruct((shards, cols, docs), BF16),
+            jax.ShapeDtypeStruct((owners, docs), F32),
+            jax.ShapeDtypeStruct((owners, docs), F32),
+            jax.ShapeDtypeStruct((PAIRS + 8, labels), F32),
+            jax.ShapeDtypeStruct((PAIRS + 8, labels), F32),
         ),
-        in_specs=[HBM] * 4,
-        out_specs=(HBM, SMEM, VMEM),
+        in_specs=[HBM] * 6,
+        out_specs=(HBM, SMEM, VMEM, VMEM, VMEM, VMEM, VMEM),
         scratch_shapes=[
             pltpu.VMEM(ids.shape, jnp.int32),
             pltpu.VMEM(used.shape, jnp.int32),
+            pltpu.VMEM(pos.shape, jnp.int32),
+            pltpu.VMEM(neg.shape, jnp.int32),
             pltpu.VMEM(code_shape, F32),
             pltpu.VMEM(values.shape, BF16),
             pltpu.VMEM(weight_t.shape, BF16),
@@ -164,10 +207,10 @@
             pltpu.SemaphoreType.DMA((groups,)),
             pltpu.SemaphoreType.DMA(()),
             pltpu.SemaphoreType.DMA(()),
-            pltpu.SemaphoreType.DMA((2,)),
+            pltpu.SemaphoreType.DMA((4,)),
         ],
-        compiler_params=pltpu.CompilerParams(vmem_limit_bytes=60 << 20),
-    )(ids, used, values, weight_t)
+        compiler_params=pltpu.CompilerParams(vmem_limit_bytes=62_500_000),
+    )(ids, used, pos, neg, values, weight_t)
 
 
 def backward_kernel(
@@ -363,50 +406,27 @@
     block_count, block_size, col_count = in_weight.shape
     doc_total, slot_count = doc_blocks.shape
     lab_count, hidden_width = out_weight.shape
-    feat_index = lax.axis_index("feat")
-    label_index = lax.axis_index("label")
     owners = lax.axis_size("label")
     shards = lax.axis_size("feat")
-
     groups = doc_total // GROUP
-    packed, chunks, copies = forward(
+    packed, chunks, copies, base, pairs, pos_count, neg_count = forward(
         doc_blocks.T,
-        doc_counts.reshape(1, doc_total),
+        doc_counts,
+        pos_labels.T,
+        neg_labels.T,
         doc_values.reshape(groups, GROUP * slot_count, block_size),
         jnp.swapaxes(in_weight, 1, 2),
         shards,
-    )
-
-    labels_t = jnp.concatenate([pos_labels.T, neg_labels.T], axis=0)
-    rel = labels_t // lab_count - feat_index * owners
-    count = jnp.sum(
-        (rel[None] == jnp.arange(owners, dtype=jnp.int32)[:, None, None]).astype(F32), axis=1
-    )
-    docs = jnp.arange(doc_total, dtype=jnp.int32)
-    before = (docs[:, None] < docs[None, :]).astype(BF16)
-    base = jnp.dot(count.astype(BF16), before, preferred_element_type=F32)
-    place = jnp.where(count > 0, base, -1.0)
-    spot = jnp.arange(PAIRS + 8, dtype=jnp.int32)
-    ranks = spot // 8 * QUARTER + spot % QUARTER + spot % 8 // QUARTER * (PAIRS // 2)
-    ranks = jnp.where(spot < PAIRS, ranks, -2).astype(F32)
-    nt = NT
+        owners,
+        lab_count,
+    )
+    place = jnp.where(pairs > 0, base, -1.0)
     arrived = lax.all_to_all(copies, "feat", 0, 0, tiled=True)
     row_shape = (owners, QUARTER, PAIRS * col_count // QUARTER)
     pre_t, sent = local_call(
         hidden_kernel, (arrived, place), (copies.shape[1:], F32), (row_shape, BF16)
     )
     got = lax.all_to_all(sent, "label", 0, 0, tiled=True)
-
-    own = labels_t - (feat_index * owners + label_index) * lab_count
-    own = jnp.where((own >= 0) & (own < lab_count), own + 1, 0).astype(BF16)
-    own_place = lax.dynamic_slice_in_dim(place, label_index, 1, 0)
-    own_pick = (own_place == ranks[:, None]).astype(BF16)
-    row_labels = lax.dot_general(own_pick, own, nt, preferred_element_type=F32)
-    names = jnp.arange(1, lab_count + 1, dtype=jnp.int32).astype(F32)
-    hits = (row_labels[:, :, None] == names[None, None, :]).astype(F32)
-    pos_slots = pos_labels.shape[1]
-    pos_count = jnp.sum(hits[:, :pos_slots], axis=1)
-    neg_count = jnp.sum(hits[:, pos_slots:], axis=1)
     back, rows, label_grad = local_call(
         label_kernel,
         (got, out_weight, pos_count, neg_count),

time: 101 us -> 99.2 us (0.982)
  blocking collectives: 18.3 us -> 52.6 us
  starting transfers between devices: 31.2 us -> 11.3 us
  waiting for transfers between devices: 35.2 us -> 20.9 us
  local copies, waits for them, and re-layouts: 1.29 us -> 0.02 us
    all_to_all x0 -> x1, blocking collectives: none -> 34.4 us  [on_device(): got = lax.all_to_all(sent, 'label', 0, 0, tiled=True)]
    all_to_all x1 -> x0, starting transfers between devices: 19.8 us -> none  [on_device(): got = lax.all_to_all(sent, 'label', 0, 0, tiled=True)]
    all_to_all x1 -> x0, waiting for transfers between devices: 14.2 us -> none  [on_device(): got = lax.all_to_all(sent, 'label', 0, 0, tiled=True)]
    reshape x1 -> x0, local copies, waits for them, and re-layouts: 1.25 us -> none  [on_device(): doc_counts.reshape(1, doc_total)]
  transfers between devices with their start and end apart: 3 -> 2, of which waited for: 3 -> 2; matrix products, arithmetic and copies ran while one was open for 2% -> 2% of each run, Pallas kernels for 0% -> 0%
where the time goes in v4:
time: 99.2 us; the launch traced here: 98.5 us
  blocking collectives  52.6 us (53%)
  waiting for transfers between devices  20.9 us (21%)
  starting transfers between devices  11.3 us (11%)
  Pallas kernels  10.7 us (11%)
  matrix products  1.42 us (1%)
    all_to_all x1, blocking collectives, on_device(): got = lax.all_to_all(sent, 'label', 0, 0, tiled=True)  34.4 us
    all_to_all x1, blocking collectives, on_device(): came = lax.all_to_all(back, 'label', 0, 0, tiled=True)  18.2 us
    all_to_all x1, waiting for transfers between devices, on_device(): parts = lax.all_to_all(copies, 'feat', 0, 0, tiled=True)  11 us
    all_to_all x1, waiting for transfers between devices, on_device(): arrived = lax.all_to_all(copies, 'feat', 0, 0, tiled=True)  9.88 us
    all_to_all x1, starting transfers between devices, on_device(): arrived = lax.all_to_all(copies, 'feat', 0, 0, tiled=True)  7.73 us
    pallas_call x1, Pallas kernels, forward(): pl.pallas_call(functools.partial(forward_kernel, owners=owners, labels=la...  5.63 us
    all_to_all x1, starting transfers between devices, on_device(): parts = lax.all_to_all(copies, 'feat', 0, 0, tiled=True)  3.61 us
    pallas_call x3, Pallas kernels, local_call(): pl.pallas_call(kernel, out_shape=tuple((jax.ShapeDtypeStruct(shape, kind)...  2.67 us
  transfers between devices with their start and end apart: 2, of which 2 were waited for; matrix products, arithmetic and copies ran while one was open for 2% of the time, Pallas kernels for 0%

profile of v4, /device:TPU:1, one launch (start us, length us, event | category | flops | bytes accessed | tf_op | source)
XLA Modules:
  0.0 98.5 jit_solution(11511082140541871132)
XLA Ops:
  0.6 5.6 %shard_map.86 = (bf16[12,272,256]{2,1,0:T(8,128)(2,1)}, s32[1,1]{1,0:T(1,128)}, bf16[16,64,384]{2,1,0:T(8,128)(2,1)}, f32[32,384]{1,0:T(8,128)}, f32[32,384]{1,0...) custom-call(s32[8,384]{1,0:T(8,128)} %bitcast.12, s32[384]{0:T(512)} %used_hbm.1, s32[8,384]{1,0:T(8,128)} %bitcast.13, ...), custom_call_target="tpu_custom_call" | custom-call | tf_op jit(solution)/shard_map/pallas_call | solution.py:183
  6.3 0.0 copy-start.1
  6.3 0.0 copy-start.2
  6.3 0.0 copy-start.3
  6.3 7.7 %all-to-all-start = ((bf16[16,64,384]{2,1,0:T(8,128)(2,1)}), bf16[16,64,384]{2,1,0:T(8,128)(2,1)S(1)}, u32[]{:S(2)}, u32[]{:S(2)}) async-start(bf16[16,64,384]{2,1,0:T(8,128)(2,1)} %get-tuple-element.15), calls=%async_computation | async-start | bytes 1572864 | tf_op jit(solution)/shard_map/all_to_all | solution.py:424
  14.0 0.8 compare_select_fusion.place_ref
  14.9 9.9 %all-to-all-done.parts_ref = bf16[16,64,384]{2,1,0:T(8,128)(2,1)S(1)} async-done(((bf16[16,64,384]{2,1,0:T(8,128)(2,1)}), bf16[16,64,384]{2,1,0:T(8,128)(2,1)S(1)}, u32[]{:S(2)}, u32[]{:S(2)}) %all-to-all-start) | async-done | bytes 786464 | tf_op jit(solution)/shard_map/all_to_all | solution.py:424
  24.7 0.4 shard_map.87
  25.2 34.4 %all_to_all.20.got_ref = bf16[32,4,384]{2,1,0:T(4,128)(2,1)S(1)} all-to-all(bf16[32,4,384]{2,1,0:T(4,128)(2,1)S(1)} %get-tuple-element.18), channel_id=1, replica_groups=mesh['feat'=16,'label'=32] {'label'}, dimensions={0} | all-to-all | bytes 196608 | tf_op jit(solution)/shard_map/all_to_all | solution.py:429
  59.6 0.0 copy-done.1
  59.6 0.0 copy-done.2
  59.6 0.0 copy-done.3
  59.6 1.0 shard_map.88
  60.6 18.2 %all_to_all.21.came_ref = bf16[32,4,384]{2,1,0:T(4,128)(2,1)S(1)} all-to-all(bf16[32,4,384]{2,1,0:T(4,128)(2,1)S(1)} %get-tuple-element.21), channel_id=1, replica_groups=mesh['feat'=16,'label'=32] {'label'}, dimensions={0} | all-to-all | bytes 196608 | tf_op jit(solution)/shard_map/all_to_all | solution.py:437
  78.7 0.0 copy-start
  78.7 1.3 %shard_map.89 = bf16[16,64,384]{2,1,0:T(8,128)(2,1)} custom-call(bf16[32,4,384]{2,1,0:T(4,128)(2,1)S(1)} %all_to_all.21.came_ref, f32[32,384]{1,0:T(8,128)S(1)} %compare_select_fusion.place_ref), custom_call_target="tpu_custom_call" | custom-call | tf_op jit(solution)/shard_map/pallas_call | solution.py:396
  80.0 3.6 %all-to-all-start.3 = ((bf16[16,64,384]{2,1,0:T(8,128)(2,1)}), bf16[16,64,384]{2,1,0:T(8,128)(2,1)S(1)}, u32[]{:S(2)}, u32[]{:S(2)}) async-start(bf16[16,64,384]{2,1,0:T(8,128)(2,1)} %shard_map.89), calls=%async_computation.3 | async-start | bytes 1572864 | tf_op jit(solution)/shard_map/all_to_all | solution.py:439
  83.6 1.4 %convolution_convert_fusion = bf16[256,2048]{1,0:T(8,128)(2,1)} fusion(bf16[32,256]{1,0:T(8,128)(2,1)S(1)} %get-tuple-element.24, bf16[32,2048]{1,0:T(8,128)(2,1)S(1)} %get-tuple-element.25), kind=kOutput, calls=%fused_computation | convolution fusion | flops 34078720 | bytes 1196032 | tf_op jit(solution)/shard_map/dot_general | solution.py:440
  85.1 11.0 %all-to-all-done.3.parts_ref = bf16[16,64,384]{2,1,0:T(8,128)(2,1)S(1)} async-done(((bf16[16,64,384]{2,1,0:T(8,128)(2,1)}), bf16[16,64,384]{2,1,0:T(8,128)(2,1)S(1)}, u32[]{:S(2)}, u32[]{:S(2)}) %all-to-all-start.3) | async-done | bytes 786464 | tf_op jit(solution)/shard_map/all_to_all | solution.py:439
  96.1 0.0 copy-done
  96.1 2.4 %shard_map.90 = bf16[32,64,256]{2,1,0:T(8,128)(2,1)} custom-call(s32[1,1]{1,0:T(1,128)} %get-tuple-element.14.count_ref, bf16[16,64,384]{2,1,0:T(8,128)(2,1)S(1)} %all-to-all-done.3.parts_ref, f32[64,384]{1,0:T(8,128)S(1)} %get-tuple-element.22.pre_ref, bf16[12,272,256]{2,1,0:T(8,128)(2,1)S(1)} %copy-done), custom_call_target="tpu_custom_call" | custom-call | tf_op jit(solution)/shard_map/pallas_call | solution.py:280
Async XLA Ops:
  6.3 53.3 %copy-start.1 = (bf16[256,2048]{1,0:T(8,128)(2,1)S(1)}, bf16[256,2048]{1,0:T(8,128)(2,1)}, u32[]{:S(2)}) copy-start(bf16[256,2048]{1,0:T(8,128)(2,1)} %weight_ref.1) | copy-start | bytes 3145732
  6.3 53.3 %copy-start.2 = (f32[32,256]{1,0:T(8,128)S(1)}, f32[32,256]{1,0:T(8,128)}, u32[]{:S(2)}) copy-start(f32[32,256]{1,0:T(8,128)} %get-tuple-element.19.pos_ref) | copy-start | bytes 98308
  6.3 53.3 %copy-start.3 = (f32[32,256]{1,0:T(8,128)S(1)}, f32[32,256]{1,0:T(8,128)}, u32[]{:S(2)}) copy-start(f32[32,256]{1,0:T(8,128)} %get-tuple-element.20.neg_ref) | copy-start | bytes 98308
  6.3 18.4 %all-to-all-start = ((bf16[16,64,384]{2,1,0:T(8,128)(2,1)}), bf16[16,64,384]{2,1,0:T(8,128)(2,1)S(1)}, u32[]{:S(2)}, u32[]{:S(2)}) async-start(bf16[16,64,384]{2,1,0:T(8,128)(2,1)} %get-tuple-element.15), calls=%async_computation | async-start | bytes 1572864 | tf_op jit(solution)/shard_map/all_to_all | solution.py:424
  78.7 17.3 %copy-start = (bf16[12,272,256]{2,1,0:T(8,128)(2,1)S(1)}, bf16[12,272,256]{2,1,0:T(8,128)(2,1)}, u32[]{:S(2)}) copy-start(bf16[12,272,256]{2,1,0:T(8,128)(2,1)} %get-tuple-element.23.packed_hbm) | copy-start | bytes 5013508
  80.0 16.0 %all-to-all-start.3 = ((bf16[16,64,384]{2,1,0:T(8,128)(2,1)}), bf16[16,64,384]{2,1,0:T(8,128)(2,1)S(1)}, u32[]{:S(2)}, u32[]{:S(2)}) async-start(bf16[16,64,384]{2,1,0:T(8,128)(2,1)} %shard_map.89), calls=%async_computation.3 | async-start | bytes 1572864 | tf_op jit(solution)/shard_map/all_to_all | solution.py:439

commit v5 on v4

--- a/solution.py
+++ b/solution.py
@@ -68,9 +68,9 @@
 
 def forward_kernel(
     ids_hbm, used_hbm, pos_hbm, neg_hbm, values_hbm, weight_hbm,
-    packed_hbm, count_ref, out_ref, base_ref, pairs_ref, pos_ref, neg_ref,
+    packed_hbm, first_ref, count_ref, out_ref, base_ref, pairs_ref, pos_ref, neg_ref,
     ids_ref, used_ref, pos_ids, neg_ids, code_ref, values, weight, rank_ref, stage, total_ref,
-    sems, weight_sem, stage_sem, id_sems, *, owners, labels,
+    values_sem, weight_sem, stage_sem, id_sems, *, owners, labels,
 ):
     groups = values.shape[0]
     blocks, cols, width = weight.shape
@@ -81,18 +81,15 @@
         pltpu.make_async_copy(pos_hbm, pos_ids, id_sems.at[2]),
         pltpu.make_async_copy(neg_hbm, neg_ids, id_sems.at[3]),
     ]
-    for load in id_loads:
-        load.start()
-    loads = [
-        pltpu.make_async_copy(values_hbm.at[g], values.at[g], sems.at[g]) for g in range(groups)
-    ]
-    for load in loads:
-        load.start()
+    for id_load in id_loads:
+        id_load.start()
+    load = pltpu.make_async_copy(values_hbm, values, values_sem)
+    load.start()
     weight_load = pltpu.make_async_copy(weight_hbm, weight, weight_sem)
     weight_load.start()
 
-    for load in id_loads:
-        load.wait()
+    for id_load in id_loads:
+        id_load.wait()
     slots, _ = ids_ref.shape
     lanes = GROUP * slots
     local = ids_ref[...] - lax.axis_index("feat") * blocks
@@ -127,8 +124,10 @@
     note_row = iota((NOTES, lanes), 0)
     lane_doc = (iota((NOTES, lanes), 1) // (lanes // GROUP)).astype(F32)
 
-    def add_chunk(chunk, wait):
+    def add_chunk(chunk, stage, wait):
         spots = (iota((CHUNK, 1), 0) + chunk * CHUNK).astype(F32)
+        if wait:
+            load.wait()
         rows = jnp.zeros((CHUNK, width), F32)
         notes = jnp.zeros((NOTES, CHUNK), F32)
         for g in range(groups):
@@ -137,13 +136,9 @@
             told = jnp.where(note_row == 1, lane_doc, told)
             told = jnp.where(note_row == 2, float(g), told).astype(BF16)
             notes += lax.dot_general(told, pick, NT, preferred_element_type=F32)
-            if wait:
-                loads[g].wait()
             rows += jnp.dot(pick, values[g], preferred_element_type=F32)
         stage[:CHUNK] = rows.astype(BF16)
         stage[CHUNK:] = notes.astype(BF16)
-        save = pltpu.make_async_copy(stage, packed_hbm.at[chunk], stage_sem)
-        save.start()
         doc_rows, block = owner_rows(stage[CHUNK:], docs)
         if wait:
             weight_load.wait()
@@ -158,16 +153,18 @@
         both = lax.dot_general(
             jnp.concatenate([high, low], axis=0), doc_rows, NT, preferred_element_type=F32
         )
-        save.wait()
         return both[:cols] + both[cols:]
 
-    total_ref[...] = add_chunk(0, True)
+    total_ref[...] = add_chunk(0, first_ref, True)
 
     @pl.when(chunks > 1)
     def _():
         @pl.loop(1, chunks)
         def _(chunk):
-            total_ref[...] += add_chunk(chunk, False)
+            total_ref[...] += add_chunk(chunk, stage, False)
+            save = pltpu.make_async_copy(stage, packed_hbm.at[chunk - 1], stage_sem)
+            save.start()
+            save.wait()
 
     part = total_ref[...].astype(BF16)
     for shard in range(out_ref.shape[0]):
@@ -183,7 +180,8 @@
     return pl.pallas_call(
         functools.partial(forward_kernel, owners=owners, labels=labels),
         out_shape=(
-            jax.ShapeDtypeStruct((most, CHUNK + NOTES, width), BF16),
+            jax.ShapeDtypeStruct((most - 1, CHUNK + NOTES, width), BF16),
+            jax.ShapeDtypeStruct((CHUNK + NOTES, width), BF16),
             jax.ShapeDtypeStruct((1, 1), jnp.int32),
             jax.ShapeDtypeStruct((shards, cols, docs), BF16),
             jax.ShapeDtypeStruct((owners, docs), F32),
@@ -192,7 +190,7 @@
             jax.ShapeDtypeStruct((PAIRS + 8, labels), F32),
         ),
         in_specs=[HBM] * 6,
-        out_specs=(HBM, SMEM, VMEM, VMEM, VMEM, VMEM, VMEM),
+        out_specs=(HBM, VMEM, SMEM, VMEM, VMEM, VMEM, VMEM, VMEM),
         scratch_shapes=[
             pltpu.VMEM(ids.shape, jnp.int32),
             pltpu.VMEM(used.shape, jnp.int32),
@@ -204,7 +202,7 @@
             pltpu.VMEM(code_shape, F32),
             pltpu.VMEM((CHUNK + NOTES, width), BF16),
             pltpu.VMEM((cols, docs), F32),
-            pltpu.SemaphoreType.DMA((groups,)),
+            pltpu.SemaphoreType.DMA(()),
             pltpu.SemaphoreType.DMA(()),
             pltpu.SemaphoreType.DMA(()),
             pltpu.SemaphoreType.DMA((4,)),
@@ -214,27 +212,24 @@
 
 
 def backward_kernel(
-    count_ref, parts_ref, pre_ref, packed_hbm, out_hbm, stage, grad_ref, total_ref, held, sem, sems
+    count_ref, parts_ref, pre_ref, first_ref, packed_hbm, out_hbm, stage, grad_ref, total_ref, held, sem, sems
 ):
     blocks, cols, width = held.shape
     docs = pre_ref.shape[1]
     chunks = count_ref[0, 0]
-    first = pltpu.make_async_copy(packed_hbm.at[0], stage, sem)
-    first.start()
     hidden_grad = parts_ref[0].astype(F32)
     for shard in range(1, parts_ref.shape[0]):
         hidden_grad += parts_ref[shard].astype(F32)
     pre = pre_ref[...]
     gate = jax.nn.sigmoid(pre)
     grad_ref[...] = (hidden_grad * gate * (1.0 + pre * (1.0 - gate))).astype(BF16)
-    first.wait()
     step = blocks // PIECES
 
-    def slot_grads():
+    def slot_grads(stage):
         doc_rows, block = owner_rows(stage[CHUNK:], docs)
         return jnp.dot(grad_ref[...], doc_rows, preferred_element_type=F32), block
 
-    def product(grads, block, piece):
+    def product(stage, grads, block, piece):
         own = [
             jnp.where(block == float(b), grads, 0.0).astype(BF16)
             for b in range(piece * step, (piece + 1) * step)
@@ -255,32 +250,36 @@
 
     @pl.when(chunks <= 1)
     def _():
-        grads, block = slot_grads()
-        finish(lambda piece: product(grads, block, piece))
+        grads, block = slot_grads(first_ref)
+        finish(lambda piece: product(first_ref, grads, block, piece))
 
     @pl.when(chunks > 1)
     def _():
+        def add(stage):
+            grads, block = slot_grads(stage)
+            for piece in range(PIECES):
+                total_ref[pl.ds(piece * step, step)] += product(stage, grads, block, piece)
+
         total_ref[...] = jnp.zeros_like(total_ref)
-
-        @pl.loop(0, chunks)
+        add(first_ref)
+
+        @pl.loop(1, chunks)
         def _(chunk):
-            later = pltpu.make_async_copy(packed_hbm.at[chunk], stage, sem)
+            later = pltpu.make_async_copy(packed_hbm.at[chunk - 1], stage, sem)
             later.start()
             later.wait()
-            grads, block = slot_grads()
-            for piece in range(PIECES):
-                total_ref[pl.ds(piece * step, step)] += product(grads, block, piece)
+            add(stage)
 
         finish(lambda piece: total_ref[pl.ds(piece * step, step)])
 
 
-def backward(count, parts, pre_t, packed, blocks):
+def backward(count, parts, pre_t, first, packed, blocks):
     cols, docs = pre_t.shape
     width = packed.shape[2]
     return pl.pallas_call(
         backward_kernel,
         out_shape=jax.ShapeDtypeStruct((blocks, cols, width), BF16),
-        in_specs=[SMEM, VMEM, VMEM, HBM],
+        in_specs=[SMEM, VMEM, VMEM, VMEM, HBM],
         out_specs=HBM,
         scratch_shapes=[
             pltpu.VMEM(packed.shape[1:], BF16),
@@ -291,7 +290,7 @@
             pltpu.SemaphoreType.DMA((PIECES,)),
         ],
         compiler_params=pltpu.CompilerParams(vmem_limit_bytes=16 << 20),
-    )(count, parts, pre_t, packed)
+    )(count, parts, pre_t, first, packed)
 
 
 def row_picks(place_ref):
@@ -409,7 +408,7 @@
     owners = lax.axis_size("label")
     shards = lax.axis_size("feat")
     groups = doc_total // GROUP
-    packed, chunks, copies, base, pairs, pos_count, neg_count = forward(
+    packed, first, chunks, copies, base, pairs, pos_count, neg_count = forward(
         doc_blocks.T,
         doc_counts,
         pos_labels.T,
@@ -440,7 +439,7 @@
     out_grad = lax.dot_general(
         label_grad, rows, (((0,), (0,)), ((), ())), preferred_element_type=F32
     ).astype(BF16)
-    in_grad = backward(chunks, parts, pre_t, packed, block_count)
+    in_grad = backward(chunks, parts, pre_t, first, packed, block_count)
     return (jnp.swapaxes(in_grad, 1, 2), out_grad)
 
 

time: 99.2 us -> 98 us (0.988)
  Pallas kernels: 10.7 us -> 9.39 us
    pallas_call x1, Pallas kernels: 5.63 us -> 4.47 us  [forward(): pl.pallas_call(functools.partial(forward_kernel, owners=owners, labels=la...]
  transfers between devices with their start and end apart: 2 -> 2, of which waited for: 2 -> 2; matrix products, arithmetic and copies ran while one was open for 2% -> 1% of each run, Pallas kernels for 0% -> 0%
where the time goes in v5:
time: 98 us; the launch traced here: 97.3 us
  blocking collectives  52.6 us (54%)
  waiting for transfers between devices  21.7 us (22%)
  starting transfers between devices  11.5 us (12%)
  Pallas kernels  9.39 us (10%)
  matrix products  1.43 us (1%)
    all_to_all x1, blocking collectives, on_device(): got = lax.all_to_all(sent, 'label', 0, 0, tiled=True)  34.4 us
    all_to_all x1, blocking collectives, on_device(): came = lax.all_to_all(back, 'label', 0, 0, tiled=True)  18.2 us
    all_to_all x1, waiting for transfers between devices, on_device(): parts = lax.all_to_all(copies, 'feat', 0, 0, tiled=True)  11 us
    all_to_all x1, waiting for transfers between devices, on_device(): arrived = lax.all_to_all(copies, 'feat', 0, 0, tiled=True)  10.7 us
    all_to_all x1, starting transfers between devices, on_device(): arrived = lax.all_to_all(copies, 'feat', 0, 0, tiled=True)  7.72 us
    pallas_call x1, Pallas kernels, forward(): pl.pallas_call(functools.partial(forward_kernel, owners=owners, labels=la...  4.47 us
    all_to_all x1, starting transfers between devices, on_device(): parts = lax.all_to_all(copies, 'feat', 0, 0, tiled=True)  3.75 us
    pallas_call x3, Pallas kernels, local_call(): pl.pallas_call(kernel, out_shape=tuple((jax.ShapeDtypeStruct(shape, kind)...  2.67 us
  transfers between devices with their start and end apart: 2, of which 2 were waited for; matrix products, arithmetic and copies ran while one was open for 1% of the time, Pallas kernels for 0%

profile of v5, /device:TPU:1, one launch (start us, length us, event | category | flops | bytes accessed | tf_op | source)
XLA Modules:
  0.0 97.3 jit_solution(14203676601727752707)
XLA Ops:
  0.6 4.5 %shard_map.86 = (bf16[11,272,256]{2,1,0:T(8,128)(2,1)}, bf16[272,256]{1,0:T(8,128)(2,1)}, s32[1,1]{1,0:T(1,128)}, bf16[16,64,384]{2,1,0:T(8,128)(2,1)}, f32[32,3...) custom-call(s32[8,384]{1,0:T(8,128)} %bitcast.12, s32[384]{0:T(512)} %used_hbm.1, ...), custom_call_target="tpu_custom_call" | custom-call | tf_op jit(solution)/shard_map/pallas_call | solution.py:180
  5.1 0.0 copy-start.5
  5.1 0.0 copy-start.6
  5.1 0.0 copy-start.1
  5.1 0.0 copy-start.3
  5.2 0.0 copy-start.4
  5.2 7.7 %all-to-all-start = ((bf16[16,64,384]{2,1,0:T(8,128)(2,1)}), bf16[16,64,384]{2,1,0:T(8,128)(2,1)S(1)}, u32[]{:S(2)}, u32[]{:S(2)}) async-start(bf16[16,64,384]{2,1,0:T(8,128)(2,1)} %get-tuple-element.16), calls=%async_computation | async-start | bytes 1572864 | tf_op jit(solution)/shard_map/all_to_all | solution.py:423
  12.9 0.0 copy-done.5
  12.9 0.0 copy-done.6
  12.9 10.7 %all-to-all-done.parts_ref = bf16[16,64,384]{2,1,0:T(8,128)(2,1)S(1)} async-done(((bf16[16,64,384]{2,1,0:T(8,128)(2,1)}), bf16[16,64,384]{2,1,0:T(8,128)(2,1)S(1)}, u32[]{:S(2)}, u32[]{:S(2)}) %all-to-all-start) | async-done | bytes 786464 | tf_op jit(solution)/shard_map/all_to_all | solution.py:423
  23.6 0.4 shard_map.87
  24.0 34.4 %all_to_all.20.got_ref = bf16[32,4,384]{2,1,0:T(4,128)(2,1)S(1)} all-to-all(bf16[32,4,384]{2,1,0:T(4,128)(2,1)S(1)} %get-tuple-element.19), channel_id=1, replica_groups=mesh['feat'=16,'label'=32] {'label'}, dimensions={0} | all-to-all | bytes 196608 | tf_op jit(solution)/shard_map/all_to_all | solution.py:428
  58.4 0.0 copy-done.1
  58.4 0.0 copy-done.3
  58.4 0.0 copy-done.4
  58.4 1.0 %shard_map.88 = (bf16[32,4,384]{2,1,0:T(4,128)(2,1)S(1)}, bf16[32,2048]{1,0:T(8,128)(2,1)S(1)}, bf16[32,256]{1,0:T(8,128)(2,1)S(1)}) custom-call(bf16[32,4,384]{2,1,0:T(4,128)(2,1)S(1)} %all_to_all.20.got_ref, bf16[256,2048]{1,0:T(8,128)(2,1)S(1)} %copy-done.1, f32[32,256]{1,0:T(8,128)S(1)} %copy-done.3, f32[32,256]{1,0:T(8,128)S(1)} %copy-done.4), custom_call_target="tpu_custom_call" | custom-call | tf_op jit(solution)/shard_map/pallas_call | solution.py:395
  59.4 18.2 %all_to_all.21.came_ref = bf16[32,4,384]{2,1,0:T(4,128)(2,1)S(1)} all-to-all(bf16[32,4,384]{2,1,0:T(4,128)(2,1)S(1)} %get-tuple-element.22), channel_id=1, replica_groups=mesh['feat'=16,'label'=32] {'label'}, dimensions={0} | all-to-all | bytes 196608 | tf_op jit(solution)/shard_map/all_to_all | solution.py:436
  77.6 1.3 %shard_map.89 = bf16[16,64,384]{2,1,0:T(8,128)(2,1)} custom-call(bf16[32,4,384]{2,1,0:T(4,128)(2,1)S(1)} %all_to_all.21.came_ref, f32[32,384]{1,0:T(8,128)S(1)} %compare_select_fusion.place_ref), custom_call_target="tpu_custom_call" | custom-call | tf_op jit(solution)/shard_map/pallas_call | solution.py:395
  78.9 3.7 %all-to-all-start.3 = ((bf16[16,64,384]{2,1,0:T(8,128)(2,1)}), bf16[16,64,384]{2,1,0:T(8,128)(2,1)S(1)}, u32[]{:S(2)}, u32[]{:S(2)}) async-start(bf16[16,64,384]{2,1,0:T(8,128)(2,1)} %shard_map.89), calls=%async_computation.3 | async-start | bytes 1572864 | tf_op jit(solution)/shard_map/all_to_all | solution.py:438
  82.6 1.4 %convolution_convert_fusion = bf16[256,2048]{1,0:T(8,128)(2,1)} fusion(bf16[32,256]{1,0:T(8,128)(2,1)S(1)} %get-tuple-element.26, bf16[32,2048]{1,0:T(8,128)(2,1)S(1)} %get-tuple-element.27), kind=kOutput, calls=%fused_computation | convolution fusion | flops 34078720 | bytes 1196032 | tf_op jit(solution)/shard_map/dot_general | solution.py:439
  84.0 11.0 %all-to-all-done.3.parts_ref = bf16[16,64,384]{2,1,0:T(8,128)(2,1)S(1)} async-done(((bf16[16,64,384]{2,1,0:T(8,128)(2,1)}), bf16[16,64,384]{2,1,0:T(8,128)(2,1)S(1)}, u32[]{:S(2)}, u32[]{:S(2)}) %all-to-all-start.3) | async-done | bytes 786464 | tf_op jit(solution)/shard_map/all_to_all | solution.py:438
  95.0 0.0 copy-done
  95.0 0.0 copy-done.2
  95.0 2.3 %shard_map.90 = bf16[32,64,256]{2,1,0:T(8,128)(2,1)} custom-call(s32[1,1]{1,0:T(1,128)} %get-tuple-element.15.count_ref, bf16[16,64,384]{2,1,0:T(8,128)(2,1)S(1)} %all-to-all-done.3.parts_ref, f32[64,384]{1,0:T(8,128)S(1)} %get-tuple-element.23.pre_ref, bf16[272,256]{1,0:T(8,128)(2,1)S(1)} %copy-done.2, bf16[11,272,256]{2,1,0:T(8,128)(2,1)S(1)} %copy-done), custom_call_target="tpu_custom_call" | custom-call | tf_op jit(solution)/shard_map/pallas_call | solution.py:279
  (3 shorter events, 0.0 us)
Async XLA Ops:
  5.1 7.8 %copy-start.5 = (f32[32,384]{1,0:T(8,128)S(1)}, f32[32,384]{1,0:T(8,128)}, u32[]{:S(2)}) copy-start(f32[32,384]{1,0:T(8,128)} %get-tuple-element.18) | copy-start | bytes 147460
  5.1 7.8 %copy-start.6 = (f32[32,384]{1,0:T(8,128)S(1)}, f32[32,384]{1,0:T(8,128)}, u32[]{:S(2)}) copy-start(f32[32,384]{1,0:T(8,128)} %get-tuple-element.17) | copy-start | bytes 147460
  5.1 53.3 %copy-start.1 = (bf16[256,2048]{1,0:T(8,128)(2,1)S(1)}, bf16[256,2048]{1,0:T(8,128)(2,1)}, u32[]{:S(2)}) copy-start(bf16[256,2048]{1,0:T(8,128)(2,1)} %weight_ref.1) | copy-start | bytes 3145732
  5.1 53.3 %copy-start.3 = (f32[32,256]{1,0:T(8,128)S(1)}, f32[32,256]{1,0:T(8,128)}, u32[]{:S(2)}) copy-start(f32[32,256]{1,0:T(8,128)} %get-tuple-element.20.pos_ref) | copy-start | bytes 98308
  5.2 53.3 %copy-start.4 = (f32[32,256]{1,0:T(8,128)S(1)}, f32[32,256]{1,0:T(8,128)}, u32[]{:S(2)}) copy-start(f32[32,256]{1,0:T(8,128)} %get-tuple-element.21.neg_ref) | copy-start | bytes 98308
  5.2 18.4 %all-to-all-start = ((bf16[16,64,384]{2,1,0:T(8,128)(2,1)}), bf16[16,64,384]{2,1,0:T(8,128)(2,1)S(1)}, u32[]{:S(2)}, u32[]{:S(2)}) async-start(bf16[16,64,384]{2,1,0:T(8,128)(2,1)} %get-tuple-element.16), calls=%async_computation | async-start | bytes 1572864 | tf_op jit(solution)/shard_map/all_to_all | solution.py:423
  78.9 16.2 %copy-start = (bf16[11,272,256]{2,1,0:T(8,128)(2,1)S(1)}, bf16[11,272,256]{2,1,0:T(8,128)(2,1)}, u32[]{:S(2)}) copy-start(bf16[11,272,256]{2,1,0:T(8,128)(2,1)} %get-tuple-element.25.packed_hbm) | copy-start | bytes 4595716
  78.9 16.2 %copy-start.2 = (bf16[272,256]{1,0:T(8,128)(2,1)S(1)}, bf16[272,256]{1,0:T(8,128)(2,1)}, u32[]{:S(2)}) copy-start(bf16[272,256]{1,0:T(8,128)(2,1)} %get-tuple-element.24.first_ref) | copy-start | bytes 417796
  78.9 16.2 %all-to-all-start.3 = ((bf16[16,64,384]{2,1,0:T(8,128)(2,1)}), bf16[16,64,384]{2,1,0:T(8,128)(2,1)S(1)}, u32[]{:S(2)}, u32[]{:S(2)}) async-start(bf16[16,64,384]{2,1,0:T(8,128)(2,1)} %shard_map.89), calls=%async_computation.3 | async-start | bytes 1572864 | tf_op jit(solution)/shard_map/all_to_all | solution.py:438

commit v6 on v5

--- a/solution.py
+++ b/solution.py
@@ -435,10 +435,11 @@
     )
     came = lax.all_to_all(back, "label", 0, 0, tiled=True)
     (copies,) = local_call(collect_kernel, (came, place), (copies.shape, BF16))
-    parts = lax.all_to_all(copies, "feat", 0, 0, tiled=True)
     out_grad = lax.dot_general(
         label_grad, rows, (((0,), (0,)), ((), ())), preferred_element_type=F32
     ).astype(BF16)
+    copies, out_grad = lax.optimization_barrier((copies, out_grad))
+    parts = lax.all_to_all(copies, "feat", 0, 0, tiled=True)
     in_grad = backward(chunks, parts, pre_t, first, packed, block_count)
     return (jnp.swapaxes(in_grad, 1, 2), out_grad)
 

time: 98 us -> 97.4 us (level)
  blocking collectives: 52.6 us -> 49.1 us
  waiting for transfers between devices: 21.7 us -> 23.5 us
  starting transfers between devices: 11.5 us -> 12.5 us
    all_to_all x1, blocking collectives: 18.2 us -> 14.7 us  [on_device(): parts = lax.all_to_all(copies, 'feat', 0, 0, tiled=True)]
    all_to_all x1, waiting for transfers between devices: 11 us -> 12.8 us  [on_device(): came = lax.all_to_all(back, 'label', 0, 0, tiled=True)]
    all_to_all x1, starting transfers between devices: 3.75 us -> 4.79 us  [on_device(): came = lax.all_to_all(back, 'label', 0, 0, tiled=True)]
where the time goes in v6:
time: 97.4 us; the launch traced here: 96.4 us
  blocking collectives  49.1 us (50%)
  waiting for transfers between devices  23.5 us (24%)
  starting transfers between devices  12.5 us (13%)
  Pallas kernels  9.09 us (9%)
  matrix products  1.43 us (1%)
    all_to_all x1, blocking collectives, on_device(): got = lax.all_to_all(sent, 'label', 0, 0, tiled=True)  34.4 us
    all_to_all x1, blocking collectives, on_device(): parts = lax.all_to_all(copies, 'feat', 0, 0, tiled=True)  14.7 us
    all_to_all x1, waiting for transfers between devices, on_device(): came = lax.all_to_all(back, 'label', 0, 0, tiled=True)  12.8 us
    all_to_all x1, waiting for transfers between devices, on_device(): arrived = lax.all_to_all(copies, 'feat', 0, 0, tiled=True)  10.7 us
    all_to_all x1, starting transfers between devices, on_device(): arrived = lax.all_to_all(copies, 'feat', 0, 0, tiled=True)  7.72 us
    all_to_all x1, starting transfers between devices, on_device(): came = lax.all_to_all(back, 'label', 0, 0, tiled=True)  4.79 us
    pallas_call x1, Pallas kernels, forward(): pl.pallas_call(functools.partial(forward_kernel, owners=owners, labels=la...  4.47 us
    pallas_call x3, Pallas kernels, local_call(): pl.pallas_call(kernel, out_shape=tuple((jax.ShapeDtypeStruct(shape, kind)...  2.42 us
  transfers between devices with their start and end apart: 2, of which 2 were waited for; matrix products, arithmetic and copies ran while one was open for 1% of the time, Pallas kernels for 0%

profile of v6, /device:TPU:1, one launch (start us, length us, event | category | flops | bytes accessed | tf_op | source)
XLA Modules:
  0.0 96.4 jit_solution(105769744415463051)
XLA Ops:
  0.6 4.5 %shard_map.86 = (bf16[11,272,256]{2,1,0:T(8,128)(2,1)}, bf16[272,256]{1,0:T(8,128)(2,1)}, s32[1,1]{1,0:T(1,128)}, bf16[16,64,384]{2,1,0:T(8,128)(2,1)}, f32[32,3...) custom-call(s32[8,384]{1,0:T(8,128)} %bitcast.12, s32[384]{0:T(512)} %used_hbm.1, ...), custom_call_target="tpu_custom_call" | custom-call | tf_op jit(solution)/shard_map/pallas_call | solution.py:180
  5.1 0.0 copy-start.5
  5.1 0.0 copy-start.6
  5.1 0.0 copy-start.1
  5.1 0.0 copy-start.3
  5.1 0.0 copy-start.4
  5.2 7.7 %all-to-all-start = ((bf16[16,64,384]{2,1,0:T(8,128)(2,1)}), bf16[16,64,384]{2,1,0:T(8,128)(2,1)S(1)}, u32[]{:S(2)}, u32[]{:S(2)}) async-start(bf16[16,64,384]{2,1,0:T(8,128)(2,1)} %get-tuple-element.18), calls=%async_computation | async-start | bytes 1572864 | tf_op jit(solution)/shard_map/all_to_all | solution.py:423
  12.9 0.0 copy-done.5
  12.9 0.0 copy-done.6
  12.9 10.7 %all-to-all-done.parts_ref = bf16[16,64,384]{2,1,0:T(8,128)(2,1)S(1)} async-done(((bf16[16,64,384]{2,1,0:T(8,128)(2,1)}), bf16[16,64,384]{2,1,0:T(8,128)(2,1)S(1)}, u32[]{:S(2)}, u32[]{:S(2)}) %all-to-all-start) | async-done | bytes 786464 | tf_op jit(solution)/shard_map/all_to_all | solution.py:423
  23.6 0.4 shard_map.87
  24.0 34.4 %all_to_all.20.got_ref = bf16[32,4,384]{2,1,0:T(4,128)(2,1)S(1)} all-to-all(bf16[32,4,384]{2,1,0:T(4,128)(2,1)S(1)} %get-tuple-element.21), channel_id=1, replica_groups=mesh['feat'=16,'label'=32] {'label'}, dimensions={0} | all-to-all | bytes 196608 | tf_op jit(solution)/shard_map/all_to_all | solution.py:428
  58.4 0.0 copy-done.1
  58.4 0.0 copy-done.3
  58.4 0.0 copy-done.4
  58.4 1.6 %shard_map.88 = (bf16[32,4,384]{2,1,0:T(4,128)(2,1)}, bf16[32,2048]{1,0:T(8,128)(2,1)S(1)}, bf16[32,256]{1,0:T(8,128)(2,1)S(1)}) custom-call(bf16[32,4,384]{2,1,0:T(4,128)(2,1)S(1)} %all_to_all.20.got_ref, bf16[256,2048]{1,0:T(8,128)(2,1)S(1)} %copy-done.1, f32[32,256]{1,0:T(8,128)S(1)} %copy-done.3, f32[32,256]{1,0:T(8,128)S(1)} %copy-done.4), custom_call_target="tpu_custom_call" | custom-call | tf_op jit(solution)/shard_map/pallas_call | solution.py:395
  60.1 4.8 %all-to-all-start.2 = ((bf16[32,4,384]{2,1,0:T(4,128)(2,1)}), bf16[32,4,384]{2,1,0:T(4,128)(2,1)S(1)}, u32[]{:S(2)}, u32[]{:S(2)}) async-start(bf16[32,4,384]{2,1,0:T(4,128)(2,1)} %get-tuple-element.24), calls=%async_computation.2 | async-start | bytes 196608 | tf_op jit(solution)/shard_map/all_to_all | solution.py:436
  64.9 0.0 copy-start.2
  64.9 1.4 %convolution_convert_fusion = bf16[256,2048]{1,0:T(8,128)(2,1)} fusion(bf16[32,256]{1,0:T(8,128)(2,1)S(1)} %get-tuple-element.25, bf16[32,2048]{1,0:T(8,128)(2,1)S(1)} %get-tuple-element.26), kind=kOutput, calls=%fused_computation | convolution fusion | flops 34078720 | bytes 1196032 | tf_op jit(solution)/shard_map/dot_general | solution.py:438
  66.3 12.8 %all-to-all-done.2.came_ref = bf16[32,4,384]{2,1,0:T(4,128)(2,1)S(1)} async-done(((bf16[32,4,384]{2,1,0:T(4,128)(2,1)}), bf16[32,4,384]{2,1,0:T(4,128)(2,1)S(1)}, u32[]{:S(2)}, u32[]{:S(2)}) %all-to-all-start.2) | async-done | bytes 98336 | tf_op jit(solution)/shard_map/all_to_all | solution.py:436
  79.1 0.4 shard_map.89
  79.5 14.7 %all_to_all.21.parts_ref = bf16[16,64,384]{2,1,0:T(8,128)(2,1)S(1)} all-to-all(bf16[16,64,384]{2,1,0:T(8,128)(2,1)S(1)} %shard_map.89), channel_id=1, replica_groups=mesh['feat'=16,'label'=32] {'feat'}, dimensions={0} | all-to-all | bytes 1572864 | tf_op jit(solution)/shard_map/all_to_all | solution.py:442
  94.2 0.0 copy-done.2
  94.2 2.2 %shard_map.90 = bf16[32,64,256]{2,1,0:T(8,128)(2,1)} custom-call(s32[1,1]{1,0:T(1,128)} %get-tuple-element.17.count_ref, bf16[16,64,384]{2,1,0:T(8,128)(2,1)S(1)} %all_to_all.21.parts_ref, f32[64,384]{1,0:T(8,128)S(1)} %get-tuple-element.28.pre_ref, bf16[272,256]{1,0:T(8,128)(2,1)S(1)} %copy-done.2, bf16[11,272,256]{2,1,0:T(8,128)(2,1)S(1)} %copy-done), custom_call_target="tpu_custom_call" | custom-call | tf_op jit(solution)/shard_map/pallas_call | solution.py:279
  (3 shorter events, 0.0 us)
Async XLA Ops:
  5.1 7.8 %copy-start.5 = (f32[32,384]{1,0:T(8,128)S(1)}, f32[32,384]{1,0:T(8,128)}, u32[]{:S(2)}) copy-start(f32[32,384]{1,0:T(8,128)} %get-tuple-element.20) | copy-start | bytes 147460
  5.1 7.8 %copy-start.6 = (f32[32,384]{1,0:T(8,128)S(1)}, f32[32,384]{1,0:T(8,128)}, u32[]{:S(2)}) copy-start(f32[32,384]{1,0:T(8,128)} %get-tuple-element.19) | copy-start | bytes 147460
  5.1 53.3 %copy-start.1 = (bf16[256,2048]{1,0:T(8,128)(2,1)S(1)}, bf16[256,2048]{1,0:T(8,128)(2,1)}, u32[]{:S(2)}) copy-start(bf16[256,2048]{1,0:T(8,128)(2,1)} %weight_ref.1) | copy-start | bytes 3145732
  5.1 53.3 %copy-start.3 = (f32[32,256]{1,0:T(8,128)S(1)}, f32[32,256]{1,0:T(8,128)}, u32[]{:S(2)}) copy-start(f32[32,256]{1,0:T(8,128)} %get-tuple-element.22.pos_ref) | copy-start | bytes 98308
  5.1 53.3 %copy-start.4 = (f32[32,256]{1,0:T(8,128)S(1)}, f32[32,256]{1,0:T(8,128)}, u32[]{:S(2)}) copy-start(f32[32,256]{1,0:T(8,128)} %get-tuple-element.23.neg_ref) | copy-start | bytes 98308
  5.2 18.4 %all-to-all-start = ((bf16[16,64,384]{2,1,0:T(8,128)(2,1)}), bf16[16,64,384]{2,1,0:T(8,128)(2,1)S(1)}, u32[]{:S(2)}, u32[]{:S(2)}) async-start(bf16[16,64,384]{2,1,0:T(8,128)(2,1)} %get-tuple-element.18), calls=%async_computation | async-start | bytes 1572864 | tf_op jit(solution)/shard_map/all_to_all | solution.py:423
  60.1 19.1 %all-to-all-start.2 = ((bf16[32,4,384]{2,1,0:T(4,128)(2,1)}), bf16[32,4,384]{2,1,0:T(4,128)(2,1)S(1)}, u32[]{:S(2)}, u32[]{:S(2)}) async-start(bf16[32,4,384]{2,1,0:T(4,128)(2,1)} %get-tuple-element.24), calls=%async_computation.2 | async-start | bytes 196608 | tf_op jit(solution)/shard_map/all_to_all | solution.py:436
  64.9 29.3 %copy-start = (bf16[11,272,256]{2,1,0:T(8,128)(2,1)S(1)}, bf16[11,272,256]{2,1,0:T(8,128)(2,1)}, u32[]{:S(2)}) copy-start(bf16[11,272,256]{2,1,0:T(8,128)(2,1)} %get-tuple-element.30.packed_hbm) | copy-start | bytes 4595716
  64.9 29.3 %copy-start.2 = (bf16[272,256]{1,0:T(8,128)(2,1)S(1)}, bf16[272,256]{1,0:T(8,128)(2,1)}, u32[]{:S(2)}) copy-start(bf16[272,256]{1,0:T(8,128)(2,1)} %get-tuple-element.29.first_ref) | copy-start | bytes 417796
